TPU v7x, 32 devices: a whole 2x2x4 slice. The times are simulated.
32 devices in a mesh: gx: 8 (over y, x, core), gz: 4 (over z).
Axes of the slice: x: 2, y: 2, z: 4, core: 2. Of those that a mesh axis runs over, the one named last changes fastest.
Arguments:
- density: float32 [512, 8, 1024], P('gx', None, 'gz'), may hold values from 0.5 to 2
- momentum: float32 [3, 512, 8, 1024], P(None, 'gx', None, 'gz'), may hold values from -5 to 5
- energy: float32 [512, 8, 1024], P('gx', None, 'gz'), may hold values from 2 to 6
- register: float32 [5, 512, 8, 1024], P(None, 'gx', None, 'gz'), may hold values from -6 to 6
Outputs:
- state: float32 [5, 512, 8, 1024], P(None, 'gx', None, 'gz')
- register_out: float32 [5, 512, 8, 1024], P(None, 'gx', None, 'gz')
All inputs are finite; a program needn't handle non-finite values.
Results may differ from a plain program's by a relative error of at most 0.00005.
Values sent between devices are 32-bit elements; how exact they have to be, the bound alone decides.
A program may use at most 64 MiB of HBM per device.

v0:
```python
import jax
import jax.numpy as jnp
import numpy as np
from jax import lax
from jax.sharding import PartitionSpec as P

BAND = 40


lele_alpha = 0.45
coef_near = 49.0 / 60.0
coef_far = 1.0 / 15.0
step_size = 0.2


def padded(block, sides, width):
    for axis, dim in sides:
        count = lax.axis_size(axis)
        forward = [(i, i + 1) for i in range(count - 1)]
        forward.append((count - 1, 0))
        backward = [(target, source) for source, target in forward]
        low = lax.ppermute(
            lax.slice_in_dim(block, block.shape[dim] - width, None, axis=dim), axis, forward
        )
        high = lax.ppermute(lax.slice_in_dim(block, 0, width, axis=dim), axis, backward)
        block = jnp.concatenate([low, block, high], axis=dim)
    return block


def stencil_terms(extended, axis_dim):
    length = extended.shape[axis_dim] - 4
    near = lax.slice_in_dim(extended, 3, 3 + length, axis=axis_dim) - lax.slice_in_dim(
        extended, 1, 1 + length, axis=axis_dim
    )
    far = lax.slice_in_dim(extended, 4, 4 + length, axis=axis_dim) - lax.slice_in_dim(
        extended, 0, length, axis=axis_dim
    )
    return coef_near * near + coef_far * far


def band_table(count):
    root_term = (np.sqrt(1.0 - 4.0 * lele_alpha * lele_alpha) - 1.0) / (2.0 * lele_alpha)
    norm_term = 1.0 / np.sqrt(1.0 - 4.0 * lele_alpha * lele_alpha)
    rows_idx = np.arange(count)[:, None]
    cols_idx = np.arange(count + 2 * BAND)[None, :]
    distance = np.abs(rows_idx + BAND - cols_idx)
    values = np.where(distance <= BAND, norm_term * np.power(root_term, distance), 0.0)
    return jnp.asarray(values, jnp.float32)


def along_x(rows_data, table):
    return jnp.einsum("ij,fjyz->fiyz", table, rows_data, precision=lax.Precision.HIGHEST)


def along_z(rows_data, table):
    return jnp.einsum("fxyj,ij->fxyi", rows_data, table, precision=lax.Precision.HIGHEST)


def per_device(density, momentum, energy, register):
    inverse_rho = 1.0 / density
    moment_x = momentum[0]
    moment_y = momentum[1]
    moment_z = momentum[2]
    pressure = 0.4 * (
        energy
        - 0.5 * (moment_x * moment_x + moment_y * moment_y + moment_z * moment_z) * inverse_rho
    )
    velocity_x = moment_x * inverse_rho
    velocity_z = moment_z * inverse_rho
    enthalpy = energy + pressure
    flux_x = jnp.stack(
        [
            moment_x,
            moment_x * velocity_x + pressure,
            moment_y * velocity_x,
            moment_z * velocity_x,
            enthalpy * velocity_x,
        ]
    )
    flux_z = jnp.stack(
        [
            moment_z,
            moment_x * velocity_z,
            moment_y * velocity_z,
            moment_z * velocity_z + pressure,
            enthalpy * velocity_z,
        ]
    )
    cells_x = flux_x.shape[1]
    cells_z = flux_z.shape[3]
    extended_x = padded(flux_x, (("gx", 1),), BAND + 2)
    deriv_x = along_x(stencil_terms(extended_x, 1), band_table(cells_x))
    extended_z = padded(flux_z, (("gz", 3),), BAND + 2)
    deriv_z = along_z(stencil_terms(extended_z, 3), band_table(cells_z))
    rate = -(deriv_x + deriv_z)
    register_out = -(5.0 / 9.0) * register + step_size * rate
    fields = jnp.concatenate([density[None], momentum, energy[None]], axis=0)
    state = fields + 15.0 / 16.0 * register_out
    return (state, register_out)


def solution(mesh):
    in_specs = (
        P("gx", None, "gz"),
        P(None, "gx", None, "gz"),
        P("gx", None, "gz"),
        P(None, "gx", None, "gz"),
    )
    out_specs = (P(None, "gx", None, "gz"), P(None, "gx", None, "gz"))
    return jax.shard_map(
        per_device, mesh=mesh, in_specs=in_specs, out_specs=out_specs, check_vma=False
    )
```

profile of v0, /device:TPU:0, one launch (start us, length us, event | category | flops | bytes accessed | tf_op | source)
XLA Modules:
  0.0 86.5 jit_solution(11277872572517786595)
XLA Ops:
  0.6 0.0 copy-start
  0.6 1.4 %slice_dynamic-update-slice_fusion.1 = (f32[5,64,8,256]{3,2,1,0:T(8,128)S(1)}, f32[5,64,8,256]{3,2,1,0:T(8,128)S(1)}) fusion(f32[3,64,8,256]{3,2,1,0:T(8,128)} %param.7), kind=kLoop, calls=%fused_computation.52 | loop fusion | bytes 2097152
  2.0 0.3 copy-done
  2.4 1.5 %bitcast_dynamic-update-slice_fusion.7 = (f32[5,64,8,256]{3,2,1,0:T(8,128)S(1)}, f32[64,8,256]{2,1,0:T(8,128)S(1)}, f32[64,8,256]{2,1,0:T(8,128)S(1)}, f32[5,64,8,256]{3,2,1,0:T(8,128)S(1)}, f32[64,8,256]{2,1,0:T(8,128)S(1)}) fusion(f32[5,64,8,256]{3,2,1,0:T(8,128)S(1)} %get-tuple-element.25, f32[3,64,8,256]{3,2,1,0:T(8,128)S(1)} %copy-done, ...), kind=kLoop, calls=%fused_computation.29 | loop fusion | flops 1966080 | bytes 5242880
  3.8 0.0 copy-start.6
  3.8 0.1 bitcast_dynamic-update-slice_fusion.6
  3.9 0.1 bitcast_dynamic-update-slice_fusion.5
  4.1 0.8 copy-done.6
  4.9 0.1 bitcast_dynamic-update-slice_fusion.4
  5.0 0.0 copy-start.1
  5.0 0.0 copy-start.3
  5.0 2.2 %fusion.23 = (f32[5,42,8,256]{3,2,1,0:T(8,128)}, f32[5,42,8,256]{3,2,1,0:T(8,128)}) fusion(f32[5,64,8,256]{3,2,1,0:T(8,128)S(1)} %get-tuple-element.27), kind=kLoop, calls=%fused_computation.54 | loop fusion | bytes 6881280 | tf_op jit(solution)/shard_map/slice | solution.py:23
  7.3 0.3 copy-done.1
  7.5 0.5 collective-permute-start
  8.0 2.9 %collective-permute-start.1 = (f32[5,42,8,256]{3,2,1,0:T(8,128)}, f32[5,42,8,256]{3,2,1,0:T(8,128)}, u32[]{:S(2)}, u32[]{:S(2)}) collective-permute-start(f32[5,42,8,256]{3,2,1,0:T(8,128)} %get-tuple-element.16), channel_id=1, source_target_pairs={{4,0},{8,4},{12,8},{16,12},{20,16},{24,20},{28,24},{0,28},{5,1},{9... | collective-permute-start | bytes 5160968 | tf_op jit(solution)/shard_map/ppermute | solution.py:25
  10.9 0.0 copy-done.3
  10.9 1.5 %fusion.24 = (f32[5,64,8,42]{3,2,1,0:T(8,128)}, f32[5,64,8,42]{3,2,1,0:T(8,128)S(1)}) fusion(f32[5,64,8,256]{3,2,1,0:T(8,128)S(1)} %get-tuple-element.28), kind=kLoop, calls=%fused_computation.55 | loop fusion | bytes 1720320 | tf_op jit(solution)/shard_map/slice | solution.py:23
  12.4 2.8 %copy.36 = f32[5,64,8,42]{1,2,3,0:T(8,128)} copy(f32[5,64,8,42]{3,2,1,0:T(8,128)} %get-tuple-element.17) | data formatting | bytes 860160 | tf_op jit(solution)/shard_map/slice | solution.py:23
  15.2 2.3 %collective-permute-start.2 = (f32[5,64,8,42]{1,2,3,0:T(8,128)}, f32[5,64,8,42]{1,2,3,0:T(8,128)}, u32[]{:S(2)}, u32[]{:S(2)}) collective-permute-start(f32[5,64,8,42]{1,2,3,0:T(8,128)} %copy.36), channel_id=1, source_target_pairs={{0,1},{1,2},{2,3},{3,0},{4,5},{5,6},{6,7},{7,4},{8,9},{9,10},{10,1... | collective-permute-start | bytes 1290248 | tf_op jit(solution)/shard_map/ppermute | solution.py:22
  17.5 1.4 %copy.37 = f32[5,64,8,42]{1,2,3,0:T(8,128)} copy(f32[5,64,8,42]{3,2,1,0:T(8,128)S(1)} %get-tuple-element.18) | data formatting | bytes 860160 | tf_op jit(solution)/shard_map/slice | solution.py:25
  18.9 0.0 copy-start.8
  18.9 2.0 %collective-permute-start.3 = (f32[5,64,8,42]{1,2,3,0:T(8,128)}, f32[5,64,8,42]{1,2,3,0:T(8,128)S(1)}, u32[]{:S(2)}, u32[]{:S(2)}) collective-permute-start(f32[5,64,8,42]{1,2,3,0:T(8,128)} %copy.37), channel_id=1, source_target_pairs={{1,0},{2,1},{3,2},{0,3},{5,4},{6,5},{7,6},{4,7},{9,8},{10,9},{11,1... | collective-permute-start | bytes 1290248 | tf_op jit(solution)/shard_map/ppermute | solution.py:25
  21.0 1.7 %copy.33 = f32[3,64,8,256]{3,1,2,0:T(8,128)} copy(f32[3,64,8,256]{3,2,1,0:T(8,128)S(1)} %copy-done) | data formatting | bytes 3145728 | tf_op args[1]
  22.7 0.0 copy-done.8
  22.7 1.3 %copy_bitcast_fusion = (f32[1,64,8,256]{3,1,2,0:T(8,128)}, f32[1,64,8,256]{3,1,2,0:T(8,128)}) fusion(f32[64,8,256]{2,1,0:T(8,128)S(1)} %copy-done.6, f32[64,8,256]{2,1,0:T(8,128)S(1)} %copy-done.8), kind=kLoop, calls=%fused_computation.49 | loop fusion | bytes 2097152 | tf_op jit(solution)/shard_map/broadcast_in_dim | solution.py:97
  24.0 0.0 copy-start.4
  24.0 15.9 %collective-permute-done.2 = f32[5,64,8,42]{1,2,3,0:T(8,128)} collective-permute-done((f32[5,64,8,42]{1,2,3,0:T(8,128)}, f32[5,64,8,42]{1,2,3,0:T(8,128)}, u32[]{:S(2)}, u32[]{:S(2)}) %collective-permute-start.2) | collective-permute-done | bytes 430112 | tf_op jit(solution)/shard_map/ppermute | solution.py:22
  39.9 2.7 %copy.38 = f32[5,64,8,42]{3,2,1,0:T(8,128)} copy(f32[5,64,8,42]{1,2,3,0:T(8,128)} %collective-permute-done.2) | data formatting | bytes 860160 | tf_op jit(solution)/shard_map/ppermute | solution.py:22
  42.6 13.8 %collective-permute-done.3 = f32[5,64,8,42]{1,2,3,0:T(8,128)S(1)} collective-permute-done((f32[5,64,8,42]{1,2,3,0:T(8,128)}, f32[5,64,8,42]{1,2,3,0:T(8,128)S(1)}, u32[]{:S(2)}, u32[]{:S(2)}) %collective-permute-start.3) | collective-permute-done | bytes 430112 | tf_op jit(solution)/shard_map/ppermute | solution.py:25
  56.4 1.6 %copy.39 = f32[5,64,8,42]{3,2,1,0:T(8,128)} copy(f32[5,64,8,42]{1,2,3,0:T(8,128)S(1)} %collective-permute-done.3) | data formatting | bytes 860160 | tf_op jit(solution)/shard_map/ppermute | solution.py:25
  58.0 0.0 copy-done.4
  58.0 3.1 %pad_maximum_fusion.1 = f32[5,64,8,340]{3,2,1,0:T(8,128)S(1)} fusion(f32[5,64,8,42]{3,2,1,0:T(8,128)} %copy.39, f32[5,64,8,256]{3,2,1,0:T(8,128)S(1)} %copy-done.4, f32[5,64,8,42]{3,2,1,0:T(8,128)} %copy.38), kind=kLoop, calls=%fused_computation.13 | loop fusion | flops 1740800 | bytes 6963200 | tf_op jit(solution)/shard_map/concatenate | solution.py:26
  61.1 0.0 copy-start.2
  61.1 3.1 %fusion.6 = f32[5,64,8,336]{3,2,1,0:T(8,128)S(1)} fusion(f32[5,64,8,340]{3,2,1,0:T(8,128)S(1)} %pad_maximum_fusion.1), kind=kLoop, calls=%fused_computation.10 | loop fusion | flops 4300800 | bytes 17203200 | tf_op jit(solution)/shard_map/add | solution.py:38
  64.2 0.0 collective-permute-done
  64.2 0.0 collective-permute-done.1
  64.2 0.0 copy-done.2
  64.2 2.4 %pad_maximum_fusion = f32[5,148,8,256]{3,2,1,0:T(8,128)S(1)} fusion(f32[5,42,8,256]{3,2,1,0:T(8,128)} %collective-permute-done.1, f32[5,64,8,256]{3,2,1,0:T(8,128)S(1)} %copy-done.2, f32[5,42,8,256]{3,2,1,0:T(8,128)} %collective-permute-done), kind=kLoop, calls=%fused_computation | loop fusion | flops 3031040 | bytes 12124160 | tf_op jit(solution)/shard_map/concatenate | solution.py:26
  66.7 0.0 copy-start.12
  66.7 2.5 %fusion.1 = f32[5,144,8,256]{3,2,1,0:T(8,128)S(1)} fusion(f32[5,148,8,256]{3,2,1,0:T(8,128)S(1)} %pad_maximum_fusion), kind=kLoop, calls=%fused_computation.3 | loop fusion | flops 7372800 | bytes 29491200 | tf_op jit(solution)/shard_map/add | solution.py:38
  69.2 0.0 copy-done.12
  69.2 0.0 copy-start.5
  69.2 0.0 copy-start.7
  69.2 0.0 copy-start.9
  69.2 0.0 copy-start.10
  69.2 0.0 copy-start.11
  69.3 5.2 %fusion.3 = f32[5,8,256,64]{2,3,1,0:T(8,128)S(1)} fusion(f32[64,144,1,1]{1,0,3,2:T(8,128)S(1)} %copy-done.12, f32[5,144,8,256]{3,2,1,0:T(8,128)S(1)} %fusion.1), kind=kOutput, calls=%fused_computation.6 | convolution fusion | flops 1132462080 | bytes 8556544 | tf_op jit(solution)/shard_map/ij,fjyz->fiyz/dot_general | solution.py:52
  74.4 0.0 copy-done.5
  74.4 0.0 copy-done.7
  74.4 0.0 copy-done.9
  74.4 0.0 copy-done.10
  74.5 0.0 copy-done.11
  74.5 6.0 %maximum_add_fusion = (f32[5,64,8,256]{3,1,2,0:T(8,128)S(1)}, f32[5,64,8,256]{3,1,2,0:T(8,128)S(1)}) fusion(f32[1,64,8,256]{3,1,2,0:T(8,128)S(1)} %copy-done.9, f32[3,64,8,256]{3,1,2,0:T(8,128)S(1)} %copy-done.5, f32[1,64,8,256]{3,1,2,0:T(8,128)S(1)} %copy-done.10, f32[5,8,256,64]{2,3,1,0:T(8,128)S(1)} %fusion.3, f32[5,64,8,256]{3,2,1,0:T(8,128)S(1)} %copy-done.7, ...), kind=kOutput, calls=%fused_computation.16 | convolution fusion | flops 2648309760 | bytes 16891904 | tf_op jit(solution)/shard_map/fxyj,ij->fxyi/dot_general | solution.py:56
  80.5 3.0 %copy.41 = f32[5,64,8,256]{3,2,1,0:T(8,128)} copy(f32[5,64,8,256]{3,1,2,0:T(8,128)S(1)} %get-tuple-element.8) | data formatting | bytes 5242880
  83.5 3.0 %copy.42 = f32[5,64,8,256]{3,2,1,0:T(8,128)} copy(f32[5,64,8,256]{3,1,2,0:T(8,128)S(1)} %get-tuple-element.9) | data formatting | bytes 5242880
Async XLA Ops:
  0.6 1.7 %copy-start = (f32[3,64,8,256]{3,2,1,0:T(8,128)S(1)}, f32[3,64,8,256]{3,2,1,0:T(8,128)}, u32[]{:S(2)}) copy-start(f32[3,64,8,256]{3,2,1,0:T(8,128)} %param.7) | copy-start | bytes 4718596
  3.8 1.0 %copy-start.6 = (f32[64,8,256]{2,1,0:T(8,128)S(1)}, f32[64,8,256]{2,1,0:T(8,128)}, u32[]{:S(2)}) copy-start(f32[64,8,256]{2,1,0:T(8,128)} %param.8) | copy-start | bytes 1572868
  5.0 2.5 %copy-start.1 = (f32[5,64,8,256]{3,2,1,0:T(8,128)}, f32[5,64,8,256]{3,2,1,0:T(8,128)S(1)}, u32[]{:S(2)}) copy-start(f32[5,64,8,256]{3,2,1,0:T(8,128)S(1)} %get-tuple-element.27) | copy-start | bytes 7864324
  5.0 5.9 %copy-start.3 = (f32[5,64,8,256]{3,2,1,0:T(8,128)}, f32[5,64,8,256]{3,2,1,0:T(8,128)S(1)}, u32[]{:S(2)}) copy-start(f32[5,64,8,256]{3,2,1,0:T(8,128)S(1)} %get-tuple-element.28) | copy-start | bytes 7864324
  7.5 56.7 %collective-permute-start = (f32[5,42,8,256]{3,2,1,0:T(8,128)}, f32[5,42,8,256]{3,2,1,0:T(8,128)}, u32[]{:S(2)}, u32[]{:S(2)}) collective-permute-start(f32[5,42,8,256]{3,2,1,0:T(8,128)} %get-tuple-element.15), channel_id=1, source_target_pairs={{0,4},{4,8},{8,12},{12,16},{16,20},{20,24},{24,28},{28,0},{1,5},{5... | collective-permute-start | bytes 5160968 | tf_op jit(solution)/shard_map/ppermute | solution.py:22
  8.0 56.2 %collective-permute-start.1 = (f32[5,42,8,256]{3,2,1,0:T(8,128)}, f32[5,42,8,256]{3,2,1,0:T(8,128)}, u32[]{:S(2)}, u32[]{:S(2)}) collective-permute-start(f32[5,42,8,256]{3,2,1,0:T(8,128)} %get-tuple-element.16), channel_id=1, source_target_pairs={{4,0},{8,4},{12,8},{16,12},{20,16},{24,20},{28,24},{0,28},{5,1},{9... | collective-permute-start | bytes 5160968 | tf_op jit(solution)/shard_map/ppermute | solution.py:25
  15.2 24.8 %collective-permute-start.2 = (f32[5,64,8,42]{1,2,3,0:T(8,128)}, f32[5,64,8,42]{1,2,3,0:T(8,128)}, u32[]{:S(2)}, u32[]{:S(2)}) collective-permute-start(f32[5,64,8,42]{1,2,3,0:T(8,128)} %copy.36), channel_id=1, source_target_pairs={{0,1},{1,2},{2,3},{3,0},{4,5},{5,6},{6,7},{7,4},{8,9},{9,10},{10,1... | collective-permute-start | bytes 1290248 | tf_op jit(solution)/shard_map/ppermute | solution.py:22
  18.9 3.8 %copy-start.8 = (f32[64,8,256]{2,1,0:T(8,128)S(1)}, f32[64,8,256]{2,1,0:T(8,128)}, u32[]{:S(2)}) copy-start(f32[64,8,256]{2,1,0:T(8,128)} %param.6) | copy-start | bytes 1572868
  18.9 37.5 %collective-permute-start.3 = (f32[5,64,8,42]{1,2,3,0:T(8,128)}, f32[5,64,8,42]{1,2,3,0:T(8,128)S(1)}, u32[]{:S(2)}, u32[]{:S(2)}) collective-permute-start(f32[5,64,8,42]{1,2,3,0:T(8,128)} %copy.37), channel_id=1, source_target_pairs={{1,0},{2,1},{3,2},{0,3},{5,4},{6,5},{7,6},{4,7},{9,8},{10,9},{11,1... | collective-permute-start | bytes 1290248 | tf_op jit(solution)/shard_map/ppermute | solution.py:25
  24.0 34.0 %copy-start.4 = (f32[5,64,8,256]{3,2,1,0:T(8,128)S(1)}, f32[5,64,8,256]{3,2,1,0:T(8,128)}, u32[]{:S(2)}) copy-start(f32[5,64,8,256]{3,2,1,0:T(8,128)} %copy-done.3) | copy-start | bytes 7864324
  61.1 3.1 %copy-start.2 = (f32[5,64,8,256]{3,2,1,0:T(8,128)S(1)}, f32[5,64,8,256]{3,2,1,0:T(8,128)}, u32[]{:S(2)}) copy-start(f32[5,64,8,256]{3,2,1,0:T(8,128)} %copy-done.1) | copy-start | bytes 7864324
  66.7 2.5 %copy-start.12 = (f32[64,144,1,1]{1,0,3,2:T(8,128)S(1)}, f32[64,144,1,1]{1,0,3,2:T(8,128)}, u32[]{:S(2)}) copy-start(f32[64,144,1,1]{1,0,3,2:T(8,128)} %constant.24) | copy-start | bytes 110596
  69.2 5.2 %copy-start.5 = (f32[3,64,8,256]{3,1,2,0:T(8,128)S(1)}, f32[3,64,8,256]{3,1,2,0:T(8,128)}, u32[]{:S(2)}) copy-start(f32[3,64,8,256]{3,1,2,0:T(8,128)} %copy.33) | copy-start | bytes 4718596
  69.2 5.2 %copy-start.7 = (f32[5,64,8,256]{3,2,1,0:T(8,128)S(1)}, f32[5,64,8,256]{3,2,1,0:T(8,128)}, u32[]{:S(2)}) copy-start(f32[5,64,8,256]{3,2,1,0:T(8,128)} %param.9) | copy-start | bytes 7864324
  69.2 5.2 %copy-start.9 = (f32[1,64,8,256]{3,1,2,0:T(8,128)S(1)}, f32[1,64,8,256]{3,1,2,0:T(8,128)}, u32[]{:S(2)}) copy-start(f32[1,64,8,256]{3,1,2,0:T(8,128)} %get-tuple-element.29) | copy-start | bytes 1572868
  69.2 5.2 %copy-start.10 = (f32[1,64,8,256]{3,1,2,0:T(8,128)S(1)}, f32[1,64,8,256]{3,1,2,0:T(8,128)}, u32[]{:S(2)}) copy-start(f32[1,64,8,256]{3,1,2,0:T(8,128)} %get-tuple-element.30) | copy-start | bytes 1572868
  69.2 5.2 %copy-start.11 = (f32[256,336,1,1]{0,1,3,2:T(8,128)S(1)}, f32[256,336,1,1]{0,1,3,2:T(8,128)}, u32[]{:S(2)}) copy-start(f32[256,336,1,1]{0,1,3,2:T(8,128)} %constant.25) | copy-start | bytes 1032196
where the time goes:
time: 86.8 us; the launch traced here: 86.5 us
  waiting for transfers between devices  29.7 us (34%)
  local copies, waits for them, and re-layouts  24 us (28%)
  other arithmetic  13 us (15%)
  matrix products  11.2 us (13%)
  starting transfers between devices  7.7 us (9%)
    ppermute x2, waiting for transfers between devices, padded(): lax.ppermute(lax.slice_in_dim(block, block.shape[dim] - width, None, axis...  15.9 us
    ppermute x2, waiting for transfers between devices, padded(): lax.ppermute(lax.slice_in_dim(block, 0, width, axis=dim), axis, backward)  13.8 us
    unnamed x30, local copies, waits for them, and re-layouts  10.5 us
    slice x3, local copies, waits for them, and re-layouts, padded(): lax.slice_in_dim(block, block.shape[dim] - width, None, axis=dim)  6.53 us
    dot_general x1, matrix products, along_z(): jnp.einsum('fxyj,ij->fxyi', rows_data, table, precision=lax.Precision.HIG...  6.02 us
    add x2, other arithmetic, stencil_terms(): return coef_near * near + coef_far * far  5.59 us
    concatenate x2, other arithmetic, padded(): block = jnp.concatenate([low, block, high], axis=dim)  5.56 us
    dot_general x1, matrix products, along_x(): jnp.einsum('ij,fjyz->fiyz', table, rows_data, precision=lax.Precision.HIG...  5.15 us
  transfers between devices with their start and end apart: 4, of which 2 were waited for; matrix products, arithmetic and copies ran while one was open for 22% of the time, Pallas kernels for 0%

commit v1 on v0

v1 whole, which is shorter than its diff:
```python
import functools

import jax
import jax.numpy as jnp
import numpy as np
from jax import lax
from jax.experimental import pallas as pl
from jax.experimental.pallas import tpu as pltpu
from jax.sharding import PartitionSpec as P

ALPHA = 0.45
NEAR = 49.0 / 60.0
FAR = 1.0 / 15.0
STEP = 0.2
CHUNK = 16

ROOT = (np.sqrt(1.0 - 4.0 * ALPHA * ALPHA) - 1.0) / (2.0 * ALPHA)
NORM = 1.0 / np.sqrt(1.0 - 4.0 * ALPHA * ALPHA)
GEOM = NORM * (NEAR * (1.0 / ROOT - ROOT) + FAR * (ROOT**-2 - ROOT**2))
EXTRA = NORM * FAR * (ROOT - 1.0 / ROOT)
SUM_COEF = -STEP * GEOM * ROOT
DIFF_COEF = -STEP * EXTRA


def split(values):
    high = np.asarray(values, np.float32).astype(jnp.bfloat16)
    low = (np.asarray(values, np.float64) - high.astype(np.float64)).astype(jnp.bfloat16)
    return high, low


def summary_table(count):
    cols = np.arange(count)
    rows = np.zeros((4, count))
    rows[0] = ROOT ** (count - 1 - cols)
    rows[1, count - 1] = 1.0
    rows[2] = ROOT**cols
    rows[3, 0] = 1.0
    high, low = split(rows)
    out = np.zeros((16, count), jnp.bfloat16)
    out[0:4] = high
    out[4:8] = low
    return out


def correction_table(count):
    cols = np.arange(count)
    rows = np.zeros((4, count))
    rows[0] = -SUM_COEF * ROOT**cols
    rows[1, 0] = -DIFF_COEF
    rows[2] = SUM_COEF * ROOT ** (count - 1 - cols)
    rows[3, count - 1] = DIFF_COEF
    high, low = split(rows)
    out = np.zeros((16, count), jnp.bfloat16)
    out[0:4] = high
    out[4:8] = high
    out[8:12] = low
    return out


def local_table(count):
    offset = np.arange(count)[:, None] - np.arange(count)[None, :]
    reach = np.abs(offset)
    values = SUM_COEF * np.power(ROOT, np.maximum(reach - 1, 0)) + DIFF_COEF * (reach == 1)
    return split(np.sign(offset) * values)


def weight_table(chunks):
    out = np.zeros((chunks, chunks + 3), np.float32)
    for c in range(chunks):
        for k in range(c + 1, chunks):
            out[c, k] = ROOT ** ((k - c - 1) * CHUNK)
        out[c, chunks] = ROOT ** ((chunks - 1 - c) * CHUNK)
        out[c, chunks + 1] = ROOT ** (c * CHUNK)
        out[c, chunks + 2] = 1.0 if c > 0 else 0.0
    return out


def fluxes(rho, mx, my, mz, energy):
    inverse = 1.0 / rho
    vx = mx * inverse
    vz = mz * inverse
    pressure = 0.4 * (energy - 0.5 * (mx * mx + my * my + mz * mz) * inverse)
    total = energy + pressure
    fx = (mx, mx * vx + pressure, my * vx, mz * vx, total * vx)
    fz = (mz, mx * vz, my * vz, mz * vz + pressure, total * vz)
    return fx, fz


def summary_kernel(w_ref, rho_ref, mom_ref, en_ref, zw_ref, b_ref, xr_ref, xl_ref, zr_ref, zl_ref):
    c = pl.program_id(0)
    fx, fz = fluxes(rho_ref[...], mom_ref[0], mom_ref[1], mom_ref[2], en_ref[...])
    carry_weight = w_ref[c, w_ref.shape[1] - 1]
    total_weight = w_ref[c, w_ref.shape[1] - 2]
    zw = zw_ref[...]
    rows = fz[0].shape[0] * fz[0].shape[1]
    for k in range(5):
        f = fx[k]
        left = jnp.where(carry_weight > 0.0, xr_ref[0, k], 0.0)
        for i in range(CHUNK):
            left = f[i] + ROOT * left
        right = f[CHUNK - 1]
        for i in range(CHUNK - 2, -1, -1):
            right = f[i] + ROOT * right
        b_ref[0, 0, k] = left
        b_ref[0, 1, k] = f[CHUNK - 1]
        b_ref[0, 2, k] = right
        b_ref[0, 3, k] = f[0]
        xr_ref[0, k] = left
        xr_ref[1, k] = f[CHUNK - 1]
        base = jnp.where(carry_weight > 0.0, xl_ref[0, k], 0.0)
        xl_ref[0, k] = base + total_weight * right
        xl_ref[1, k] = jnp.where(carry_weight > 0.0, xl_ref[1, k], f[0])

        g = fz[k].reshape(rows, fz[k].shape[2])
        high = g.astype(jnp.bfloat16)
        low = (g - high.astype(jnp.float32)).astype(jnp.bfloat16)
        dims = (((1,), (1,)), ((), ()))
        first = lax.dot_general(zw, high, dims, preferred_element_type=jnp.float32)
        second = lax.dot_general(zw, low, dims, preferred_element_type=jnp.float32)
        both = first[0:4] + first[4:8] + second[0:4]
        zr_ref[0, :, k * rows : (k + 1) * rows] = both[0:2]
        zl_ref[0, :, k * rows : (k + 1) * rows] = both[2:4]


def final_kernel(
    w_ref, rho_ref, mom_ref, en_ref, reg_ref, b_ref, xr_ref, xl_ref, zr_ref, zl_ref,
    hh_ref, hl_ref, cz_ref, state_ref, out_ref, stack_ref, left_ref,
):
    c = pl.program_id(0)
    chunks = b_ref.shape[0]
    fx, fz = fluxes(rho_ref[...], mom_ref[0], mom_ref[1], mom_ref[2], en_ref[...])
    fields = (rho_ref, mom_ref.at[0], mom_ref.at[1], mom_ref.at[2], en_ref)
    rows = fz[0].shape[0] * fz[0].shape[1]
    before = jnp.maximum(c - 1, 0)
    after = jnp.minimum(c + 1, chunks - 1)

    zr = zr_ref[0]
    zl = zl_ref[0]
    zr_high = zr.astype(jnp.bfloat16).astype(jnp.float32)
    zl_high = zl.astype(jnp.bfloat16).astype(jnp.float32)
    stack_ref[0:2] = zr_high
    stack_ref[2:4] = zl_high
    stack_ref[4:6] = zr - zr_high
    stack_ref[6:8] = zl - zl_high
    stack_ref[8:10] = zr_high
    stack_ref[10:12] = zl_high
    stack_ref[12:16] = jnp.zeros((4, stack_ref.shape[1]), jnp.float32)
    edges = stack_ref[...].astype(jnp.bfloat16)

    hh = hh_ref[...]
    hl = hl_ref[...]
    cz = cz_ref[...]
    for k in range(5):
        g = fz[k].reshape(rows, fz[k].shape[2])
        high = g.astype(jnp.bfloat16)
        low = (g - high.astype(jnp.float32)).astype(jnp.bfloat16)
        dz = jnp.dot(high, hh, preferred_element_type=jnp.float32)
        dz += jnp.dot(low, hh, preferred_element_type=jnp.float32)
        dz += jnp.dot(high, hl, preferred_element_type=jnp.float32)
        dz += lax.dot_general(
            edges[:, k * rows : (k + 1) * rows], cz, (((0,), (0,)), ((), ())),
            preferred_element_type=jnp.float32,
        )
        dz = dz.reshape(fz[k].shape)

        f = fx[k]
        left = w_ref[c, chunks + 1] * xr_ref[0, k] + w_ref[c, chunks + 2] * b_ref[before, 0, k]
        left_edge = jnp.where(c == 0, xr_ref[1, k], b_ref[before, 1, k])
        right = w_ref[c, chunks] * xl_ref[0, k]
        for m in range(1, chunks):
            right += w_ref[c, m] * b_ref[m, 2, k]
        right_edge = jnp.where(c == chunks - 1, xl_ref[1, k], b_ref[after, 3, k])
        for i in range(CHUNK):
            left_ref[i] = left
            left = f[i] + ROOT * left
        for i in range(CHUNK - 1, -1, -1):
            upper = f[i + 1] if i < CHUNK - 1 else right_edge
            lower = f[i - 1] if i > 0 else left_edge
            rate = SUM_COEF * (right - left_ref[i]) + DIFF_COEF * (upper - lower) + dz[i]
            fresh = rate - (5.0 / 9.0) * reg_ref[k, i]
            out_ref[k, i] = fresh
            state_ref[k, i] = fields[k][i] + (15.0 / 16.0) * fresh
            right = f[i] + ROOT * right


def shift(value, axis, step):
    count = lax.axis_size(axis)
    return lax.ppermute(value, axis, [(i, (i + step) % count) for i in range(count)])


def per_device(density, momentum, energy, register):
    nx, ny, nz = density.shape
    chunks = nx // CHUNK
    rows = CHUNK * ny
    f32 = jnp.float32
    plane = pl.BlockSpec((CHUNK, ny, nz), lambda c: (c, 0, 0))
    triple = pl.BlockSpec((3, CHUNK, ny, nz), lambda c: (0, c, 0, 0))
    quint = pl.BlockSpec((5, CHUNK, ny, nz), lambda c: (0, c, 0, 0))
    edge_x = pl.BlockSpec((2, 5, ny, nz), lambda c: (0, 0, 0, 0))
    edge_z = pl.BlockSpec((1, 2, 5 * rows), lambda c: (c, 0, 0))
    table = lambda shape: pl.BlockSpec(shape, lambda c: (0,) * len(shape))
    smem = pl.BlockSpec(memory_space=pltpu.SMEM)
    weights = jnp.asarray(weight_table(chunks))
    params = pltpu.CompilerParams(
        dimension_semantics=("arbitrary",), vmem_limit_bytes=40 * 1024 * 1024
    )

    bounds, xr, xl, zr, zl = pl.pallas_call(
        summary_kernel,
        grid=(chunks,),
        in_specs=[smem, plane, triple, plane, table((16, nz))],
        out_specs=[
            pl.BlockSpec((1, 4, 5, ny, nz), lambda c: (c, 0, 0, 0, 0)),
            edge_x, edge_x, edge_z, edge_z,
        ],
        out_shape=[
            jax.ShapeDtypeStruct((chunks, 4, 5, ny, nz), f32),
            jax.ShapeDtypeStruct((2, 5, ny, nz), f32),
            jax.ShapeDtypeStruct((2, 5, ny, nz), f32),
            jax.ShapeDtypeStruct((chunks, 2, 5 * rows), f32),
            jax.ShapeDtypeStruct((chunks, 2, 5 * rows), f32),
        ],
        compiler_params=params,
        name="summaries",
    )(weights, density, momentum, energy, jnp.asarray(summary_table(nz)))

    xr = shift(xr, "gx", 1)
    xl = shift(xl, "gx", -1)
    zr = shift(zr, "gz", 1)
    zl = shift(zl, "gz", -1)

    high, low = local_table(nz)
    return pl.pallas_call(
        final_kernel,
        grid=(chunks,),
        in_specs=[
            smem, plane, triple, plane, quint,
            table((chunks, 4, 5, ny, nz)), edge_x, edge_x, edge_z, edge_z,
            table((nz, nz)), table((nz, nz)), table((16, nz)),
        ],
        out_specs=[quint, quint],
        out_shape=[jax.ShapeDtypeStruct((5, nx, ny, nz), f32)] * 2,
        scratch_shapes=[
            pltpu.VMEM((16, 5 * rows), f32),
            pltpu.VMEM((CHUNK, ny, nz), f32),
        ],
        compiler_params=params,
        name="section",
    )(
        weights, density, momentum, energy, register, bounds, xr, xl, zr, zl,
        jnp.asarray(high), jnp.asarray(low), jnp.asarray(correction_table(nz)),
    )


def solution(mesh):
    specs = (
        P("gx", None, "gz"),
        P(None, "gx", None, "gz"),
        P("gx", None, "gz"),
        P(None, "gx", None, "gz"),
    )
    out = P(None, "gx", None, "gz")
    return jax.shard_map(
        per_device, mesh=mesh, in_specs=specs, out_specs=(out, out), check_vma=False
    )
```

time: 86.8 us -> 24.6 us (0.28)
  waiting for transfers between devices: 29.7 us -> 1.98 us
  local copies, waits for them, and re-layouts: 24 us -> 6.67 us
  other arithmetic: 13 us -> 0 us
  matrix products: 11.2 us -> 0 us
  Pallas kernels: 0 us -> 7.17 us
    ppermute x4, waiting for transfers between devices: 29.7 us -> 1.98 us  [shift(): lax.ppermute(value, axis, [(i, (i + step) % count) for i in range(count)])]
    dot_general x2 -> x0, matrix products: 11.2 us -> none  [the longest x1 6.02 us: along_z(): jnp.einsum('fxyj,ij->fxyi', rows_data, table, precision=lax.Precision.HIG...]
    slice x4 -> x0, local copies, waits for them, and re-layouts: 7.96 us -> none  [the longest x3 6.53 us: padded(): lax.slice_in_dim(block, block.shape[dim] - width, None, axis=dim)]
    pallas_call x0 -> x2, Pallas kernels: none -> 7.17 us  [the longest x1 4.95 us: per_device(): pl.pallas_call(final_kernel, grid=(chunks,), in_specs=[smem, plane, tripl...]
    add x2 -> x0, other arithmetic: 5.59 us -> none  [stencil_terms(): return coef_near * near + coef_far * far]
    concatenate x2 -> x0, other arithmetic: 5.56 us -> none  [padded(): block = jnp.concatenate([low, block, high], axis=dim)]
    ppermute x2 -> x0, local copies, waits for them, and re-layouts: 4.27 us -> none  [the longest x1 2.72 us: padded(): lax.ppermute(lax.slice_in_dim(block, block.shape[dim] - width, None, axis...]
    unnamed x30 -> x18, local copies, waits for them, and re-layouts: 10.5 us -> 6.67 us
  transfers between devices with their start and end apart: 4 -> 4, of which waited for: 2 -> 2; matrix products, arithmetic and copies ran while one was open for 22% -> 0% of each run, Pallas kernels for 0% -> 0%
where the time goes in v1:
time: 24.6 us; the launch traced here: 24.2 us
  starting transfers between devices  7.73 us (31%)
  Pallas kernels  7.17 us (29%)
  local copies, waits for them, and re-layouts  6.67 us (27%)
  waiting for transfers between devices  1.98 us (8%)
  between operations  0.67 us (3%)
    ppermute x4, starting transfers between devices, shift(): lax.ppermute(value, axis, [(i, (i + step) % count) for i in range(count)])  7.73 us
    unnamed x18, local copies, waits for them, and re-layouts  6.67 us
    pallas_call x1, Pallas kernels, per_device(): pl.pallas_call(final_kernel, grid=(chunks,), in_specs=[smem, plane, tripl...  4.95 us
    pallas_call x1, Pallas kernels, per_device(): pl.pallas_call(summary_kernel, grid=(chunks,), in_specs=[smem, plane, tri...  2.22 us
    ppermute x4, waiting for transfers between devices, shift(): lax.ppermute(value, axis, [(i, (i + step) % count) for i in range(count)])  1.98 us
  transfers between devices with their start and end apart: 4, of which 2 were waited for; matrix products, arithmetic and copies ran while one was open for 0% of the time, Pallas kernels for 0%

profile of v1, /device:TPU:0, one launch (start us, length us, event | category | flops | bytes accessed | tf_op | source)
XLA Modules:
  0.0 24.2 jit_solution(3736340155232249742)
XLA Ops:
  0.6 0.0 copy-start
  0.6 1.4 %copy-done = f32[3,64,8,256]{3,2,1,0:T(8,128)S(1)} copy-done((f32[3,64,8,256]{3,2,1,0:T(8,128)S(1)}, f32[3,64,8,256]{3,2,1,0:T(8,128)}, u32[]{:S(2)}) %copy-start) | copy-done | bytes 1572888
  2.0 0.0 copy-start.2
  2.0 1.0 %copy-done.2 = f32[64,8,256]{2,1,0:T(8,128)S(1)} copy-done((f32[64,8,256]{2,1,0:T(8,128)S(1)}, f32[64,8,256]{2,1,0:T(8,128)}, u32[]{:S(2)}) %copy-start.2) | copy-done | bytes 524312
  3.1 0.0 copy-start.3
  3.1 1.0 %copy-done.3 = f32[64,8,256]{2,1,0:T(8,128)S(1)} copy-done((f32[64,8,256]{2,1,0:T(8,128)S(1)}, f32[64,8,256]{2,1,0:T(8,128)}, u32[]{:S(2)}) %copy-start.3) | copy-done | bytes 524312
  4.1 0.0 copy-start.7
  4.1 0.7 %copy-done.7 = bf16[16,256]{1,0:T(8,128)(2,1)S(1)} copy-done((bf16[16,256]{1,0:T(8,128)(2,1)S(1)}, bf16[16,256]{1,0:T(8,128)(2,1)}, u32[]{:S(2)}) %copy-start.7) | copy-done | bytes 8216
  4.8 0.0 copy-start.8
  4.8 0.7 %copy-done.8 = f32[4,7]{1,0:T(4,128)S(1)} copy-done((f32[4,7]{1,0:T(4,128)S(1)}, f32[4,7]{1,0:T(4,128)}, u32[]{:S(2)}) %copy-start.8) | copy-done | bytes 136
  5.5 0.0 copy-start.1
  5.5 0.0 copy-start.6
  5.5 2.2 %summaries.1 = (f32[4,4,5,8,256]{4,3,2,1,0:T(8,128)S(1)}, f32[2,5,8,256]{3,2,1,0:T(8,128)S(1)}, f32[2,5,8,256]{3,2,1,0:T(8,128)S(1)}, f32[4,2,640]{2,1,0:T(2,128)S(1)}, f32[4,2,640]{2,1,0:T(2,128)S(1)}) custom-call(f32[4,7]{1,0:T(4,128)S(1)} %copy-done.8, f32[64,8,256]{2,1,0:T(8,128)S(1)} %copy-done.2, f32[3,64,8,256]{3,2,1,0:T(8,128)S(1)} %copy-done, ...), custom_call_target="tpu_custom_call" | custom-call | tf_op jit(solution)/shard_map/summaries/pallas_call | solution.py:208
  7.7 0.5 %collective-permute-start = (f32[2,5,8,256]{3,2,1,0:T(8,128)S(1)}, f32[2,5,8,256]{3,2,1,0:T(8,128)S(1)}, u32[]{:S(2)}, u32[]{:S(2)}) collective-permute-start(f32[2,5,8,256]{3,2,1,0:T(8,128)S(1)} %get-tuple-element.8), channel_id=1, source_target_pairs={{0,4},{4,8},{8,12},{12,16},{16,20},{20,24},{24,28},{28,0},{1,5},{5... | collective-permute-start | bytes 245768 | tf_op jit(solution)/shard_map/ppermute | solution.py:188
  8.2 2.9 %collective-permute-start.1 = (f32[2,5,8,256]{3,2,1,0:T(8,128)S(1)}, f32[2,5,8,256]{3,2,1,0:T(8,128)S(1)}, u32[]{:S(2)}, u32[]{:S(2)}) collective-permute-start(f32[2,5,8,256]{3,2,1,0:T(8,128)S(1)} %get-tuple-element.9), channel_id=1, source_target_pairs={{0,28},{4,0},{8,4},{12,8},{16,12},{20,16},{24,20},{28,24},{1,29},{... | collective-permute-start | bytes 245768 | tf_op jit(solution)/shard_map/ppermute | solution.py:188
  11.2 2.3 %collective-permute-start.2 = (f32[4,2,640]{2,1,0:T(2,128)S(1)}, f32[4,2,640]{2,1,0:T(2,128)S(1)}, u32[]{:S(2)}, u32[]{:S(2)}) collective-permute-start(f32[4,2,640]{2,1,0:T(2,128)S(1)} %get-tuple-element.10), channel_id=1, source_target_pairs={{0,1},{1,2},{2,3},{3,0},{4,5},{5,6},{6,7},{7,4},{8,9},{9,10},{10,1... | collective-permute-start | bytes 61448 | tf_op jit(solution)/shard_map/ppermute | solution.py:188
  13.4 2.0 %collective-permute-start.3 = (f32[4,2,640]{2,1,0:T(2,128)S(1)}, f32[4,2,640]{2,1,0:T(2,128)S(1)}, u32[]{:S(2)}, u32[]{:S(2)}) collective-permute-start(f32[4,2,640]{2,1,0:T(2,128)S(1)} %get-tuple-element.11), channel_id=1, source_target_pairs={{0,3},{1,0},{2,1},{3,2},{4,7},{5,4},{6,5},{7,6},{8,11},{9,8},{10,9... | collective-permute-start | bytes 61448 | tf_op jit(solution)/shard_map/ppermute | solution.py:188
  15.5 1.9 %collective-permute-done.2.zr_ref = f32[4,2,640]{2,1,0:T(2,128)S(1)} collective-permute-done((f32[4,2,640]{2,1,0:T(2,128)S(1)}, f32[4,2,640]{2,1,0:T(2,128)S(1)}, u32[]{:S(2)}, u32[]{:S(2)}) %collective-permute-start.2) | collective-permute-done | bytes 20512 | tf_op jit(solution)/shard_map/ppermute | solution.py:188
  17.3 0.1 collective-permute-done.3.zl_ref
  17.4 0.0 collective-permute-done.xr_ref
  17.4 0.0 collective-permute-done.1.xl_ref
  17.4 0.0 copy-done.1
  17.4 0.0 copy-done.6
  17.5 0.0 copy-start.4
  17.5 0.9 %copy-done.4 = bf16[256,256]{1,0:T(8,128)(2,1)S(1)} copy-done((bf16[256,256]{1,0:T(8,128)(2,1)S(1)}, bf16[256,256]{1,0:T(8,128)(2,1)}, u32[]{:S(2)}) %copy-start.4) | copy-done | bytes 131096
  18.4 0.0 copy-start.5
  18.4 0.9 %copy-done.5 = bf16[256,256]{1,0:T(8,128)(2,1)S(1)} copy-done((bf16[256,256]{1,0:T(8,128)(2,1)S(1)}, bf16[256,256]{1,0:T(8,128)(2,1)}, u32[]{:S(2)}) %copy-start.5) | copy-done | bytes 131096
  19.3 5.0 %section.1 = (f32[5,64,8,256]{3,2,1,0:T(8,128)}, f32[5,64,8,256]{3,2,1,0:T(8,128)}) custom-call(f32[4,7]{1,0:T(4,128)S(1)} %copy-done.8, f32[64,8,256]{2,1,0:T(8,128)S(1)} %copy-done.2, f32[3,64,8,256]{3,2,1,0:T(8,128)S(1)} %copy-done, f32[64,8,256]{2,1,0:T(8,128)S(1)} %copy-done.3, f32[5,64,8,256]{3,2,1,0:T(8,128)S(1)} %copy-done.1, ...), custom_call_target="tpu_custom_call" | custom-call | tf_op jit(solution)/shard_map/section/pallas_call | solution.py:233
Async XLA Ops:
  0.6 1.4 %copy-start = (f32[3,64,8,256]{3,2,1,0:T(8,128)S(1)}, f32[3,64,8,256]{3,2,1,0:T(8,128)}, u32[]{:S(2)}) copy-start(f32[3,64,8,256]{3,2,1,0:T(8,128)} %mom_ref.3) | copy-start | bytes 4718596
  2.0 1.0 %copy-start.2 = (f32[64,8,256]{2,1,0:T(8,128)S(1)}, f32[64,8,256]{2,1,0:T(8,128)}, u32[]{:S(2)}) copy-start(f32[64,8,256]{2,1,0:T(8,128)} %rho_ref.3) | copy-start | bytes 1572868
  3.1 1.0 %copy-start.3 = (f32[64,8,256]{2,1,0:T(8,128)S(1)}, f32[64,8,256]{2,1,0:T(8,128)}, u32[]{:S(2)}) copy-start(f32[64,8,256]{2,1,0:T(8,128)} %en_ref.3) | copy-start | bytes 1572868
  4.1 0.7 %copy-start.7 = (bf16[16,256]{1,0:T(8,128)(2,1)S(1)}, bf16[16,256]{1,0:T(8,128)(2,1)}, u32[]{:S(2)}) copy-start(bf16[16,256]{1,0:T(8,128)(2,1)} %constant.11.clone.zw_ref) | copy-start | bytes 24580
  4.8 0.7 %copy-start.8 = (f32[4,7]{1,0:T(4,128)S(1)}, f32[4,7]{1,0:T(4,128)}, u32[]{:S(2)}) copy-start(f32[4,7]{1,0:T(4,128)} %constant.10.clone.w_ref) | copy-start | bytes 340
  5.5 11.9 %copy-start.1 = (f32[5,64,8,256]{3,2,1,0:T(8,128)S(1)}, f32[5,64,8,256]{3,2,1,0:T(8,128)}, u32[]{:S(2)}) copy-start(f32[5,64,8,256]{3,2,1,0:T(8,128)} %reg_ref.1) | copy-start | bytes 7864324
  5.5 11.9 %copy-start.6 = (bf16[16,256]{1,0:T(8,128)(2,1)S(1)}, bf16[16,256]{1,0:T(8,128)(2,1)}, u32[]{:S(2)}) copy-start(bf16[16,256]{1,0:T(8,128)(2,1)} %constant.14.clone.cz_ref) | copy-start | bytes 24580
  7.7 9.7 %collective-permute-start = (f32[2,5,8,256]{3,2,1,0:T(8,128)S(1)}, f32[2,5,8,256]{3,2,1,0:T(8,128)S(1)}, u32[]{:S(2)}, u32[]{:S(2)}) collective-permute-start(f32[2,5,8,256]{3,2,1,0:T(8,128)S(1)} %get-tuple-element.8), channel_id=1, source_target_pairs={{0,4},{4,8},{8,12},{12,16},{16,20},{20,24},{24,28},{28,0},{1,5},{5... | collective-permute-start | bytes 245768 | tf_op jit(solution)/shard_map/ppermute | solution.py:188
  8.2 9.2 %collective-permute-start.1 = (f32[2,5,8,256]{3,2,1,0:T(8,128)S(1)}, f32[2,5,8,256]{3,2,1,0:T(8,128)S(1)}, u32[]{:S(2)}, u32[]{:S(2)}) collective-permute-start(f32[2,5,8,256]{3,2,1,0:T(8,128)S(1)} %get-tuple-element.9), channel_id=1, source_target_pairs={{0,28},{4,0},{8,4},{12,8},{16,12},{20,16},{24,20},{28,24},{1,29},{... | collective-permute-start | bytes 245768 | tf_op jit(solution)/shard_map/ppermute | solution.py:188
  11.2 6.2 %collective-permute-start.2 = (f32[4,2,640]{2,1,0:T(2,128)S(1)}, f32[4,2,640]{2,1,0:T(2,128)S(1)}, u32[]{:S(2)}, u32[]{:S(2)}) collective-permute-start(f32[4,2,640]{2,1,0:T(2,128)S(1)} %get-tuple-element.10), channel_id=1, source_target_pairs={{0,1},{1,2},{2,3},{3,0},{4,5},{5,6},{6,7},{7,4},{8,9},{9,10},{10,1... | collective-permute-start | bytes 61448 | tf_op jit(solution)/shard_map/ppermute | solution.py:188
  13.4 4.0 %collective-permute-start.3 = (f32[4,2,640]{2,1,0:T(2,128)S(1)}, f32[4,2,640]{2,1,0:T(2,128)S(1)}, u32[]{:S(2)}, u32[]{:S(2)}) collective-permute-start(f32[4,2,640]{2,1,0:T(2,128)S(1)} %get-tuple-element.11), channel_id=1, source_target_pairs={{0,3},{1,0},{2,1},{3,2},{4,7},{5,4},{6,5},{7,6},{8,11},{9,8},{10,9... | collective-permute-start | bytes 61448 | tf_op jit(solution)/shard_map/ppermute | solution.py:188
  17.5 0.9 %copy-start.4 = (bf16[256,256]{1,0:T(8,128)(2,1)S(1)}, bf16[256,256]{1,0:T(8,128)(2,1)}, u32[]{:S(2)}) copy-start(bf16[256,256]{1,0:T(8,128)(2,1)} %constant.13.clone.hl_ref) | copy-start | bytes 393220
  18.4 0.9 %copy-start.5 = (bf16[256,256]{1,0:T(8,128)(2,1)S(1)}, bf16[256,256]{1,0:T(8,128)(2,1)}, u32[]{:S(2)}) copy-start(bf16[256,256]{1,0:T(8,128)(2,1)} %constant.12.clone.hh_ref) | copy-start | bytes 393220

commit v2 on v1

--- a/solution.py
+++ b/solution.py
@@ -86,8 +86,28 @@
     return fx, fz
 
 
-def summary_kernel(w_ref, rho_ref, mom_ref, en_ref, zw_ref, b_ref, xr_ref, xl_ref, zr_ref, zl_ref):
+def summary_kernel(
+    w_ref, rho_ref, mom_ref, en_ref, zw_ref, b_ref, xr_out, xl_out, zr_out, zl_out,
+    xr_ref, xl_ref, zr_ref, zl_ref, xr_got, xl_got, zr_got, zl_got, send_sem, recv_sem,
+):
     c = pl.program_id(0)
+    last = pl.num_programs(0) - 1
+    gx, gz = lax.axis_index("gx"), lax.axis_index("gz")
+    nx, nz = lax.axis_size("gx"), lax.axis_size("gz")
+    x_next, x_prev = lax.rem(gx + 1, nx), lax.rem(gx + nx - 1, nx)
+    z_next, z_prev = lax.rem(gz + 1, nz), lax.rem(gz + nz - 1, nz)
+    neighbours = ((x_next, gz), (x_prev, gz), (gx, z_next), (gx, z_prev))
+    barrier = pltpu.get_barrier_semaphore()
+
+    @pl.when(c == 0)
+    def _():
+        for target in neighbours:
+            pl.semaphore_signal(
+                barrier, inc=1, device_id=target, device_id_type=pl.DeviceIdType.MESH
+            )
+        xr_ref[...] = jnp.zeros_like(xr_ref)
+        xl_ref[...] = jnp.zeros_like(xl_ref)
+
     fx, fz = fluxes(rho_ref[...], mom_ref[0], mom_ref[1], mom_ref[2], en_ref[...])
     carry_weight = w_ref[c, w_ref.shape[1] - 1]
     total_weight = w_ref[c, w_ref.shape[1] - 2]
@@ -95,7 +115,7 @@
     rows = fz[0].shape[0] * fz[0].shape[1]
     for k in range(5):
         f = fx[k]
-        left = jnp.where(carry_weight > 0.0, xr_ref[0, k], 0.0)
+        left = xr_ref[0, k]
         for i in range(CHUNK):
             left = f[i] + ROOT * left
         right = f[CHUNK - 1]
@@ -107,9 +127,8 @@
         b_ref[0, 3, k] = f[0]
         xr_ref[0, k] = left
         xr_ref[1, k] = f[CHUNK - 1]
-        base = jnp.where(carry_weight > 0.0, xl_ref[0, k], 0.0)
-        xl_ref[0, k] = base + total_weight * right
-        xl_ref[1, k] = jnp.where(carry_weight > 0.0, xl_ref[1, k], f[0])
+        xl_ref[0, k] = xl_ref[0, k] + total_weight * right
+        xl_ref[1, k] = xl_ref[1, k] + (1.0 - carry_weight) * f[0]
 
         g = fz[k].reshape(rows, fz[k].shape[2])
         high = g.astype(jnp.bfloat16)
@@ -118,8 +137,31 @@
         first = lax.dot_general(zw, high, dims, preferred_element_type=jnp.float32)
         second = lax.dot_general(zw, low, dims, preferred_element_type=jnp.float32)
         both = first[0:4] + first[4:8] + second[0:4]
-        zr_ref[0, :, k * rows : (k + 1) * rows] = both[0:2]
-        zl_ref[0, :, k * rows : (k + 1) * rows] = both[2:4]
+        zr_ref[c, :, k * rows : (k + 1) * rows] = both[0:2]
+        zl_ref[c, :, k * rows : (k + 1) * rows] = both[2:4]
+
+    @pl.when(c == last)
+    def _():
+        pl.semaphore_wait(barrier, 4)
+        copies = []
+        pairs = ((xr_ref, xr_got), (xl_ref, xl_got), (zr_ref, zr_got), (zl_ref, zl_got))
+        for n, (source, target) in enumerate(pairs):
+            copy = pltpu.make_async_remote_copy(
+                src_ref=source,
+                dst_ref=target,
+                send_sem=send_sem.at[n],
+                recv_sem=recv_sem.at[n],
+                device_id=neighbours[n],
+                device_id_type=pl.DeviceIdType.MESH,
+            )
+            copy.start()
+            copies.append(copy)
+        for copy in copies:
+            copy.wait()
+        xr_out[...] = xr_got[...]
+        xl_out[...] = xl_got[...]
+        zr_out[...] = zr_got[...]
+        zl_out[...] = zl_got[...]
 
 
 def final_kernel(
@@ -183,11 +225,6 @@
             right = f[i] + ROOT * right
 
 
-def shift(value, axis, step):
-    count = lax.axis_size(axis)
-    return lax.ppermute(value, axis, [(i, (i + step) % count) for i in range(count)])
-
-
 def per_device(density, momentum, energy, register):
     nx, ny, nz = density.shape
     chunks = nx // CHUNK
@@ -201,9 +238,14 @@
     table = lambda shape: pl.BlockSpec(shape, lambda c: (0,) * len(shape))
     smem = pl.BlockSpec(memory_space=pltpu.SMEM)
     weights = jnp.asarray(weight_table(chunks))
-    params = pltpu.CompilerParams(
-        dimension_semantics=("arbitrary",), vmem_limit_bytes=40 * 1024 * 1024
+    params = functools.partial(
+        pltpu.CompilerParams,
+        dimension_semantics=("arbitrary",),
+        vmem_limit_bytes=60 * 1024 * 1024,
     )
+    whole_z = pl.BlockSpec((chunks, 2, 5 * rows), lambda c: (0, 0, 0))
+    x_buffer = pltpu.VMEM((2, 5, ny, nz), f32)
+    z_buffer = pltpu.VMEM((chunks, 2, 5 * rows), f32)
 
     bounds, xr, xl, zr, zl = pl.pallas_call(
         summary_kernel,
@@ -211,7 +253,7 @@
         in_specs=[smem, plane, triple, plane, table((16, nz))],
         out_specs=[
             pl.BlockSpec((1, 4, 5, ny, nz), lambda c: (c, 0, 0, 0, 0)),
-            edge_x, edge_x, edge_z, edge_z,
+            edge_x, edge_x, whole_z, whole_z,
         ],
         out_shape=[
             jax.ShapeDtypeStruct((chunks, 4, 5, ny, nz), f32),
@@ -220,14 +262,11 @@
             jax.ShapeDtypeStruct((chunks, 2, 5 * rows), f32),
             jax.ShapeDtypeStruct((chunks, 2, 5 * rows), f32),
         ],
-        compiler_params=params,
+        scratch_shapes=[x_buffer, x_buffer, z_buffer, z_buffer] * 2
+        + [pltpu.SemaphoreType.DMA((4,)), pltpu.SemaphoreType.DMA((4,))],
+        compiler_params=params(collective_id=0, has_side_effects=True),
         name="summaries",
     )(weights, density, momentum, energy, jnp.asarray(summary_table(nz)))
-
-    xr = shift(xr, "gx", 1)
-    xl = shift(xl, "gx", -1)
-    zr = shift(zr, "gz", 1)
-    zl = shift(zl, "gz", -1)
 
     high, low = local_table(nz)
     return pl.pallas_call(
@@ -244,7 +283,7 @@
             pltpu.VMEM((16, 5 * rows), f32),
             pltpu.VMEM((CHUNK, ny, nz), f32),
         ],
-        compiler_params=params,
+        compiler_params=params(),
         name="section",
     )(
         weights, density, momentum, energy, register, bounds, xr, xl, zr, zl,

time: 24.6 us -> 19.3 us (0.78)
  Pallas kernels: 7.17 us -> 18.4 us
  starting transfers between devices: 7.73 us -> 0 us
  local copies, waits for them, and re-layouts: 6.67 us -> 0 us
  waiting for transfers between devices: 1.98 us -> 0 us
    pallas_call x1, Pallas kernels: 2.22 us -> 11.4 us  [per_device(): pl.pallas_call(summary_kernel, grid=(chunks,), in_specs=[smem, plane, tri...]
    ppermute x4 -> x0, starting transfers between devices: 7.73 us -> none  [shift(): lax.ppermute(value, axis, [(i, (i + step) % count) for i in range(count)])]
    unnamed x18 -> x0, local copies, waits for them, and re-layouts: 6.67 us -> none
    pallas_call x1, Pallas kernels: 4.95 us -> 6.97 us  [per_device(): pl.pallas_call(final_kernel, grid=(chunks,), in_specs=[smem, plane, tripl...]
    ppermute x4 -> x0, waiting for transfers between devices: 1.98 us -> none  [shift(): lax.ppermute(value, axis, [(i, (i + step) % count) for i in range(count)])]
  transfers between devices with their start and end apart: 4 -> 0, of which waited for: 2 -> 0; matrix products, arithmetic and copies ran while one was open for 0% -> 0% of each run, Pallas kernels for 0% -> 0%
where the time goes in v2:
time: 19.3 us; the launch traced here: 19 us
  Pallas kernels  18.4 us (95%)
  between operations  0.64 us (3%)
    pallas_call x1, Pallas kernels, per_device(): pl.pallas_call(summary_kernel, grid=(chunks,), in_specs=[smem, plane, tri...  11.4 us
    pallas_call x1, Pallas kernels, per_device(): pl.pallas_call(final_kernel, grid=(chunks,), in_specs=[smem, plane, tripl...  6.97 us

profile of v2, /device:TPU:0, one launch (start us, length us, event | category | flops | bytes accessed | tf_op | source)
XLA Modules:
  0.0 19.0 jit_solution(5152685864197781542)
XLA Ops:
  0.6 11.4 %summaries.1 = (f32[4,4,5,8,256]{4,3,2,1,0:T(8,128)}, f32[2,5,8,256]{3,2,1,0:T(8,128)}, f32[2,5,8,256]{3,2,1,0:T(8,128)}, f32[4,2,640]{2,1,0:T(2,128)}, f32[4,2,640]{2,1,0:T(2,128)}) custom-call(f32[4,7]{1,0:T(4,128)} %constant.10.clone.w_ref, f32[64,8,256]{2,1,0:T(8,128)} %rho_ref.3, f32[3,64,8,256]{3,2,1,0:T(8,128)} %mom_ref.3, f32[64,8,256]{2,1,0:T(8,128)} %en_ref.3, ...), custom_call_target="tpu_custom_call" | custom-call | tf_op jit(solution)/shard_map/summaries/pallas_call | solution.py:250
  12.1 7.0 %section.1 = (f32[5,64,8,256]{3,2,1,0:T(8,128)}, f32[5,64,8,256]{3,2,1,0:T(8,128)}) custom-call(f32[4,7]{1,0:T(4,128)} %constant.10.clone.w_ref, f32[64,8,256]{2,1,0:T(8,128)} %rho_ref.3, f32[3,64,8,256]{3,2,1,0:T(8,128)} %mom_ref.3, f32[64,8,256]{2,1,0:T(8,128)} %en_ref.3, f32[5,64,8,256]{3,2,1,0:T(8,128)} %reg_ref.1, ...), custom_call_target="tpu_custom_call" | custom-call | tf_op jit(solution)/shard_map/section/pallas_call | solution.py:272

commit v3 on v2

v3 whole, which is shorter than its diff:
```python
import functools

import jax
import jax.numpy as jnp
import numpy as np
from jax import lax
from jax.experimental import pallas as pl
from jax.experimental.pallas import tpu as pltpu
from jax.sharding import PartitionSpec as P

ALPHA = 0.45
NEAR = 49.0 / 60.0
FAR = 1.0 / 15.0
STEP = 0.2
CHUNK = 16

ROOT = (np.sqrt(1.0 - 4.0 * ALPHA * ALPHA) - 1.0) / (2.0 * ALPHA)
NORM = 1.0 / np.sqrt(1.0 - 4.0 * ALPHA * ALPHA)
GEOM = NORM * (NEAR * (1.0 / ROOT - ROOT) + FAR * (ROOT**-2 - ROOT**2))
EXTRA = NORM * FAR * (ROOT - 1.0 / ROOT)
SUM_COEF = -STEP * GEOM * ROOT
DIFF_COEF = -STEP * EXTRA


def split(values):
    high = np.asarray(values, np.float32).astype(jnp.bfloat16)
    low = (np.asarray(values, np.float64) - high.astype(np.float64)).astype(jnp.bfloat16)
    return high, low


def summary_table(count):
    cols = np.arange(count)
    rows = np.zeros((4, count))
    rows[0] = ROOT ** (count - 1 - cols)
    rows[1, count - 1] = 1.0
    rows[2] = ROOT**cols
    rows[3, 0] = 1.0
    high, low = split(rows)
    out = np.zeros((16, count), jnp.bfloat16)
    out[0:4] = high
    out[4:8] = low
    return out


def correction_table(count):
    cols = np.arange(count)
    rows = np.zeros((4, count))
    rows[0] = -SUM_COEF * ROOT**cols
    rows[1, 0] = -DIFF_COEF
    rows[2] = SUM_COEF * ROOT ** (count - 1 - cols)
    rows[3, count - 1] = DIFF_COEF
    high, low = split(rows)
    out = np.zeros((16, count), jnp.bfloat16)
    out[0:4] = high
    out[4:8] = high
    out[8:12] = low
    return out


def local_table(count):
    offset = np.arange(count)[:, None] - np.arange(count)[None, :]
    reach = np.abs(offset)
    values = SUM_COEF * np.power(ROOT, np.maximum(reach - 1, 0)) + DIFF_COEF * (reach == 1)
    return split(np.sign(offset) * values)


def weight_table(chunks):
    out = np.zeros((chunks, 4), np.float32)
    for c in range(chunks):
        out[c, 0] = ROOT ** (c * CHUNK)
        out[c, 1] = ROOT ** ((chunks - 1 - c) * CHUNK)
        out[c, 2] = 1.0 if c == 0 else 0.0
        out[c, 3] = 1.0 if c == chunks - 1 else 0.0
    return out


def fluxes(rho, mx, my, mz, energy):
    inverse = 1.0 / rho
    vx = mx * inverse
    vz = mz * inverse
    pressure = 0.4 * (energy - 0.5 * (mx * mx + my * my + mz * mz) * inverse)
    total = energy + pressure
    fx = (mx, mx * vx + pressure, my * vx, mz * vx, total * vx)
    fz = (mz, mx * vz, my * vz, mz * vz + pressure, total * vz)
    return fx, fz


def local_kernel(
    w_ref, rho_ref, mom_ref, en_ref, reg_ref, zw_ref, hh_ref, hl_ref,
    part_ref, xr_out, xl_out, zr_out, zl_out,
    xr_ref, xl_ref, zr_ref, zl_ref, xr_got, xl_got, zr_got, zl_got,
    fx_ref, left_ref, high_ref, low_ref, dz_ref, carry_ref, send_sem, recv_sem,
):
    step = pl.program_id(0)
    chunks = high_ref.shape[0]
    cells, width, lanes = fx_ref.shape[0] - 2, fx_ref.shape[2], fx_ref.shape[3]
    rows = CHUNK * width
    gx, gz = lax.axis_index("gx"), lax.axis_index("gz")
    nx, nz = lax.axis_size("gx"), lax.axis_size("gz")
    x_next, x_prev = lax.rem(gx + 1, nx), lax.rem(gx + nx - 1, nx)
    z_next, z_prev = lax.rem(gz + 1, nz), lax.rem(gz + nz - 1, nz)
    neighbours = ((x_next, gz), (x_prev, gz), (gx, z_next), (gx, z_prev))
    barrier = pltpu.get_barrier_semaphore()
    pairs = ((xr_ref, xr_got), (xl_ref, xl_got), (zr_ref, zr_got), (zl_ref, zl_got))

    @pl.when(step == 0)
    def _():
        for target in neighbours:
            pl.semaphore_signal(
                barrier, inc=1, device_id=target, device_id_type=pl.DeviceIdType.MESH
            )
        xr_ref[...] = jnp.zeros_like(xr_ref)
        xl_ref[...] = jnp.zeros_like(xl_ref)
        carry_ref[...] = jnp.zeros_like(carry_ref)
        fx_ref[0] = jnp.zeros((5, width, lanes), jnp.float32)
        fx_ref[cells + 1] = jnp.zeros((5, width, lanes), jnp.float32)

    @pl.when(step < chunks)
    def _():
        start = step * CHUNK
        left = [xr_ref[0, k] for k in range(5)]
        right = [None] * 5
        first = [None] * 5
        for i in range(0, CHUNK, 2):
            fx, fz = fluxes(
                rho_ref[i : i + 2], mom_ref[0, i : i + 2], mom_ref[1, i : i + 2],
                mom_ref[2, i : i + 2], en_ref[i : i + 2],
            )
            for k in range(5):
                even, odd = fx[k][0], fx[k][1]
                fx_ref[start + i + 1, k] = even
                fx_ref[start + i + 2, k] = odd
                left_ref[start + i, k] = left[k]
                left[k] = even + ROOT * left[k]
                left_ref[start + i + 1, k] = left[k]
                left[k] = odd + ROOT * left[k]
                both = ROOT**i * even + ROOT ** (i + 1) * odd
                right[k] = both if i == 0 else right[k] + both
                if i == 0:
                    first[k] = even
                if i == CHUNK - 2:
                    xr_ref[1, k] = odd
                g = fz[k].reshape(2 * width, lanes)
                high = g.astype(jnp.bfloat16)
                low = (g - high.astype(jnp.float32)).astype(jnp.bfloat16)
                at = k * rows + i * width
                high_ref[step, at : at + 2 * width] = high
                low_ref[step, at : at + 2 * width] = low
        for k in range(5):
            xr_ref[0, k] = left[k]
            xl_ref[0, k] = xl_ref[0, k] + w_ref[step, 0] * right[k]
            xl_ref[1, k] = xl_ref[1, k] + w_ref[step, 2] * first[k]
        dims = (((1,), (1,)), ((), ()))
        zw = zw_ref[...]
        one = lax.dot_general(zw, high_ref[step], dims, preferred_element_type=jnp.float32)
        two = lax.dot_general(zw, low_ref[step], dims, preferred_element_type=jnp.float32)
        total = one[0:4] + one[4:8] + two[0:4]
        zr_ref[step] = total[0:2]
        zl_ref[step] = total[2:4]

    def copy_of(n):
        return pltpu.make_async_remote_copy(
            src_ref=pairs[n][0],
            dst_ref=pairs[n][1],
            send_sem=send_sem.at[n],
            recv_sem=recv_sem.at[n],
            device_id=neighbours[n],
            device_id_type=pl.DeviceIdType.MESH,
        )

    @pl.when(step == chunks - 1)
    def _():
        pl.semaphore_wait(barrier, 4)
        for n in range(4):
            copy_of(n).start()

    @pl.when(step >= chunks)
    def _():
        chunk = 2 * chunks - 1 - step
        start = chunk * CHUNK
        high = high_ref[chunk]
        hh = hh_ref[...]
        dz = jnp.dot(high, hh, preferred_element_type=jnp.float32)
        dz += jnp.dot(low_ref[chunk], hh, preferred_element_type=jnp.float32)
        dz += jnp.dot(high, hl_ref[...], preferred_element_type=jnp.float32)
        dz_ref[...] = dz.reshape(dz_ref.shape)
        right = carry_ref[...]
        upper = fx_ref[start + CHUNK + 1]
        here = fx_ref[start + CHUNK]
        for i in range(CHUNK - 1, -1, -1):
            lower = fx_ref[start + i]
            rate = SUM_COEF * (right - left_ref[start + i]) + DIFF_COEF * (upper - lower)
            part_ref[:, i] = rate + dz_ref[:, i] - (5.0 / 9.0) * reg_ref[:, i]
            right = here + ROOT * right
            upper = here
            here = lower
        carry_ref[...] = right

    @pl.when(step == 2 * chunks - 1)
    def _():
        for n in range(4):
            copy_of(n).wait()
        xr_out[...] = xr_got[...]
        xl_out[...] = xl_got[...]
        zr_out[...] = zr_got[...]
        zl_out[...] = zl_got[...]


def final_kernel(
    w_ref, rho_ref, mom_ref, en_ref, part_ref, xr_ref, xl_ref, zr_ref, zl_ref, cz_ref,
    state_ref, out_ref, stack_ref, dz_ref,
):
    c = pl.program_id(0)
    zr = zr_ref[0]
    zl = zl_ref[0]
    zr_high = zr.astype(jnp.bfloat16).astype(jnp.float32)
    zl_high = zl.astype(jnp.bfloat16).astype(jnp.float32)
    stack_ref[0:2] = zr_high
    stack_ref[2:4] = zl_high
    stack_ref[4:6] = zr - zr_high
    stack_ref[6:8] = zl - zl_high
    stack_ref[8:10] = zr_high
    stack_ref[10:12] = zl_high
    stack_ref[12:16] = jnp.zeros((4, stack_ref.shape[1]), jnp.float32)
    dz = lax.dot_general(
        stack_ref[...].astype(jnp.bfloat16), cz_ref[...], (((0,), (0,)), ((), ())),
        preferred_element_type=jnp.float32,
    )
    dz_ref[...] = dz.reshape(dz_ref.shape)
    left = (-SUM_COEF * w_ref[c, 0]) * xr_ref[0]
    right = (SUM_COEF * w_ref[c, 1]) * xl_ref[0]
    for i in range(CHUNK):
        fresh = part_ref[:, i] + dz_ref[:, i]
        fresh += ROOT**i * left + ROOT ** (CHUNK - 1 - i) * right
        if i == 0:
            fresh -= (DIFF_COEF * w_ref[c, 2]) * xr_ref[1]
        if i == CHUNK - 1:
            fresh += (DIFF_COEF * w_ref[c, 3]) * xl_ref[1]
        out_ref[:, i] = fresh
        scaled = (15.0 / 16.0) * fresh
        state_ref[0, i] = rho_ref[i] + scaled[0]
        for k in range(3):
            state_ref[k + 1, i] = mom_ref[k, i] + scaled[k + 1]
        state_ref[4, i] = en_ref[i] + scaled[4]


def per_device(density, momentum, energy, register):
    nx, ny, nz = density.shape
    chunks = nx // CHUNK
    rows = CHUNK * ny
    f32, bf16 = jnp.float32, jnp.bfloat16
    table = lambda shape: pl.BlockSpec(shape, lambda c: (0,) * len(shape))
    smem = pl.BlockSpec(memory_space=pltpu.SMEM)
    weights = jnp.asarray(weight_table(chunks))
    params = functools.partial(
        pltpu.CompilerParams,
        dimension_semantics=("arbitrary",),
        vmem_limit_bytes=60 * 1024 * 1024,
    )
    edge_x = (2, 5, ny, nz)
    edge_z = (chunks, 2, 5 * rows)
    buffers = [pltpu.VMEM(edge_x, f32)] * 2 + [pltpu.VMEM(edge_z, f32)] * 2
    high, low = local_table(nz)

    ahead = lambda s: jnp.minimum(s, chunks - 1)
    back = lambda s: jnp.minimum(2 * chunks - 1 - s, chunks - 1)
    quint = pl.BlockSpec((5, CHUNK, ny, nz), lambda s: (0, back(s), 0, 0))
    part, xr, xl, zr, zl = pl.pallas_call(
        local_kernel,
        grid=(2 * chunks,),
        in_specs=[
            smem,
            pl.BlockSpec((CHUNK, ny, nz), lambda s: (ahead(s), 0, 0)),
            pl.BlockSpec((3, CHUNK, ny, nz), lambda s: (0, ahead(s), 0, 0)),
            pl.BlockSpec((CHUNK, ny, nz), lambda s: (ahead(s), 0, 0)),
            quint, table((16, nz)), table((nz, nz)), table((nz, nz)),
        ],
        out_specs=[quint, table(edge_x), table(edge_x), table(edge_z), table(edge_z)],
        out_shape=[
            jax.ShapeDtypeStruct(shape, f32)
            for shape in ((5, nx, ny, nz), edge_x, edge_x, edge_z, edge_z)
        ],
        scratch_shapes=buffers * 2
        + [
            pltpu.VMEM((nx + 2, 5, ny, nz), f32),
            pltpu.VMEM((nx, 5, ny, nz), f32),
            pltpu.VMEM((chunks, 5 * rows, nz), bf16),
            pltpu.VMEM((chunks, 5 * rows, nz), bf16),
            pltpu.VMEM((5, CHUNK, ny, nz), f32),
            pltpu.VMEM((5, ny, nz), f32),
            pltpu.SemaphoreType.DMA((4,)),
            pltpu.SemaphoreType.DMA((4,)),
        ],
        compiler_params=params(collective_id=0, has_side_effects=True),
        name="local_part",
    )(
        weights, density, momentum, energy, register,
        jnp.asarray(summary_table(nz)), jnp.asarray(high), jnp.asarray(low),
    )

    plane = pl.BlockSpec((CHUNK, ny, nz), lambda c: (c, 0, 0))
    triple = pl.BlockSpec((3, CHUNK, ny, nz), lambda c: (0, c, 0, 0))
    quint = pl.BlockSpec((5, CHUNK, ny, nz), lambda c: (0, c, 0, 0))
    line_z = pl.BlockSpec((1, 2, 5 * rows), lambda c: (c, 0, 0))
    return pl.pallas_call(
        final_kernel,
        grid=(chunks,),
        in_specs=[
            smem, plane, triple, plane, quint, table(edge_x), table(edge_x),
            line_z, line_z, table((16, nz)),
        ],
        out_specs=[quint, quint],
        out_shape=[jax.ShapeDtypeStruct((5, nx, ny, nz), f32)] * 2,
        scratch_shapes=[
            pltpu.VMEM((16, 5 * rows), f32),
            pltpu.VMEM((5, CHUNK, ny, nz), f32),
        ],
        compiler_params=params(),
        name="neighbour_part",
    )(
        weights, density, momentum, energy, part, xr, xl, zr, zl,
        jnp.asarray(correction_table(nz)),
    )


def solution(mesh):
    specs = (
        P("gx", None, "gz"),
        P(None, "gx", None, "gz"),
        P("gx", None, "gz"),
        P(None, "gx", None, "gz"),
    )
    out = P(None, "gx", None, "gz")
    return jax.shard_map(
        per_device, mesh=mesh, in_specs=specs, out_specs=(out, out), check_vma=False
    )
```

time: 19.3 us -> 18.9 us (0.979)
  Pallas kernels: 18.4 us -> 17.9 us
    pallas_call x1, Pallas kernels: 6.97 us -> 5.87 us  [per_device(): pl.pallas_call(final_kernel, grid=(chunks,), in_specs=[smem, plane, tripl...]
    pallas_call x1, Pallas kernels: 11.4 us -> 12 us  [per_device(): pl.pallas_call(local_kernel, grid=(2 * chunks,), in_specs=[smem, pl.Block...]
where the time goes in v3:
time: 18.9 us; the launch traced here: 18.5 us
  Pallas kernels  17.9 us (95%)
  between operations  0.64 us (3%)
    pallas_call x1, Pallas kernels, per_device(): pl.pallas_call(local_kernel, grid=(2 * chunks,), in_specs=[smem, pl.Block...  12 us
    pallas_call x1, Pallas kernels, per_device(): pl.pallas_call(final_kernel, grid=(chunks,), in_specs=[smem, plane, tripl...  5.87 us

profile of v3, /device:TPU:0, one launch (start us, length us, event | category | flops | bytes accessed | tf_op | source)
XLA Modules:
  0.0 18.5 jit_solution(4819204369337424593)
XLA Ops:
  0.6 12.0 %local_part.1 = (f32[5,64,8,256]{3,2,1,0:T(8,128)}, f32[2,5,8,256]{3,2,1,0:T(8,128)}, f32[2,5,8,256]{3,2,1,0:T(8,128)}, f32[4,2,640]{2,1,0:T(2,128)}, f32[4,2,640]{2,1,0:T(2,128)}) custom-call(f32[4,4]{1,0:T(4,128)} %constant.10.clone.w_ref, f32[64,8,256]{2,1,0:T(8,128)} %rho_ref.3, f32[3,64,8,256]{3,2,1,0:T(8,128)} %mom_ref.3, f32[64,8,256]{2,1,0:T(8,128)} %en_ref.3, ...), custom_call_target="tpu_custom_call" | custom-call | tf_op jit(solution)/shard_map/local_part/pallas_call | solution.py:268
  12.6 5.9 %neighbour_part.1 = (f32[5,64,8,256]{3,2,1,0:T(8,128)}, f32[5,64,8,256]{3,2,1,0:T(8,128)}) custom-call(f32[4,4]{1,0:T(4,128)} %constant.10.clone.w_ref, f32[64,8,256]{2,1,0:T(8,128)} %rho_ref.3, f32[3,64,8,256]{3,2,1,0:T(8,128)} %mom_ref.3, f32[64,8,256]{2,1,0:T(8,128)} %en_ref.3, f32[5,64,8,256]{3,2,1,0:T(8,128)} %get-tuple-element.7.part_ref, ...), custom_call_target="tpu_custom_call" | custom-call | tf_op jit(solution)/shard_map/neighbour_part/pallas_call | solution.py:305

commit v4 on v3

--- a/solution.py
+++ b/solution.py
@@ -1,5 +1,3 @@
-import functools
-
 import jax
 import jax.numpy as jnp
 import numpy as np
@@ -89,7 +87,8 @@
     w_ref, rho_ref, mom_ref, en_ref, reg_ref, zw_ref, hh_ref, hl_ref,
     part_ref, xr_out, xl_out, zr_out, zl_out,
     xr_ref, xl_ref, zr_ref, zl_ref, xr_got, xl_got, zr_got, zl_got,
-    fx_ref, left_ref, high_ref, low_ref, dz_ref, carry_ref, send_sem, recv_sem,
+    fx_ref, left_ref, high_ref, low_ref, dz_ref, carry_ref,
+    cell_ref, reg_buf, hh_buf, hl_buf, send_sem, recv_sem, load_sem, table_sem,
 ):
     step = pl.program_id(0)
     chunks = high_ref.shape[0]
@@ -103,8 +102,35 @@
     barrier = pltpu.get_barrier_semaphore()
     pairs = ((xr_ref, xr_got), (xl_ref, xl_got), (zr_ref, zr_got), (zl_ref, zl_got))
 
+    def loads_of(chunk, first, stop):
+        at = pl.ds(chunk * CHUNK, CHUNK)
+        ends = (
+            (rho_ref.at[at], cell_ref.at[0, at]),
+            (mom_ref.at[:, at], cell_ref.at[1:4, at]),
+            (en_ref.at[at], cell_ref.at[4, at]),
+            (reg_ref.at[:, at], reg_buf.at[:, at]),
+        )
+        return [
+            pltpu.make_async_copy(source, target, load_sem.at[chunk, n])
+            for n, (source, target) in enumerate(ends)
+            if first <= n < stop
+        ]
+
+    def table_loads():
+        return (
+            pltpu.make_async_copy(hh_ref, hh_buf, table_sem.at[0]),
+            pltpu.make_async_copy(hl_ref, hl_buf, table_sem.at[1]),
+        )
+
     @pl.when(step == 0)
     def _():
+        for chunk in range(chunks):
+            for copy in loads_of(chunk, 0, 3):
+                copy.start()
+        for copy in table_loads():
+            copy.start()
+        for chunk in range(chunks - 1, -1, -1):
+            loads_of(chunk, 3, 4)[0].start()
         for target in neighbours:
             pl.semaphore_signal(
                 barrier, inc=1, device_id=target, device_id_type=pl.DeviceIdType.MESH
@@ -118,14 +144,13 @@
     @pl.when(step < chunks)
     def _():
         start = step * CHUNK
+        for copy in loads_of(step, 0, 3):
+            copy.wait()
         left = [xr_ref[0, k] for k in range(5)]
         right = [None] * 5
         first = [None] * 5
         for i in range(0, CHUNK, 2):
-            fx, fz = fluxes(
-                rho_ref[i : i + 2], mom_ref[0, i : i + 2], mom_ref[1, i : i + 2],
-                mom_ref[2, i : i + 2], en_ref[i : i + 2],
-            )
+            fx, fz = fluxes(*(cell_ref[k, pl.ds(start + i, 2)] for k in range(5)))
             for k in range(5):
                 even, odd = fx[k][0], fx[k][1]
                 fx_ref[start + i + 1, k] = even
@@ -178,11 +203,18 @@
     def _():
         chunk = 2 * chunks - 1 - step
         start = chunk * CHUNK
+
+        @pl.when(step == chunks)
+        def _():
+            for copy in table_loads():
+                copy.wait()
+
+        loads_of(chunk, 3, 4)[0].wait()
         high = high_ref[chunk]
-        hh = hh_ref[...]
+        hh = hh_buf[...]
         dz = jnp.dot(high, hh, preferred_element_type=jnp.float32)
         dz += jnp.dot(low_ref[chunk], hh, preferred_element_type=jnp.float32)
-        dz += jnp.dot(high, hl_ref[...], preferred_element_type=jnp.float32)
+        dz += jnp.dot(high, hl_buf[...], preferred_element_type=jnp.float32)
         dz_ref[...] = dz.reshape(dz_ref.shape)
         right = carry_ref[...]
         upper = fx_ref[start + CHUNK + 1]
@@ -190,7 +222,7 @@
         for i in range(CHUNK - 1, -1, -1):
             lower = fx_ref[start + i]
             rate = SUM_COEF * (right - left_ref[start + i]) + DIFF_COEF * (upper - lower)
-            part_ref[:, i] = rate + dz_ref[:, i] - (5.0 / 9.0) * reg_ref[:, i]
+            part_ref[:, i] = rate + dz_ref[:, i] - (5.0 / 9.0) * reg_buf[:, start + i]
             right = here + ROOT * right
             upper = here
             here = lower
@@ -207,41 +239,74 @@
 
 
 def final_kernel(
-    w_ref, rho_ref, mom_ref, en_ref, part_ref, xr_ref, xl_ref, zr_ref, zl_ref, cz_ref,
-    state_ref, out_ref, stack_ref, dz_ref,
+    w_ref, rho_ref, mom_ref, en_ref, part_ref, xr_in, xl_in, zr_in, zl_in, cz_in,
+    state_out, out_out, state_ref, out_ref, xr_ref, xl_ref, zr_ref, zl_ref, cz_ref,
+    stack_ref, dz_ref, edge_sem, load_sem, store_sem,
 ):
-    c = pl.program_id(0)
-    zr = zr_ref[0]
-    zl = zl_ref[0]
-    zr_high = zr.astype(jnp.bfloat16).astype(jnp.float32)
-    zl_high = zl.astype(jnp.bfloat16).astype(jnp.float32)
-    stack_ref[0:2] = zr_high
-    stack_ref[2:4] = zl_high
-    stack_ref[4:6] = zr - zr_high
-    stack_ref[6:8] = zl - zl_high
-    stack_ref[8:10] = zr_high
-    stack_ref[10:12] = zl_high
+    chunks = zr_ref.shape[0]
+    edges = [
+        pltpu.make_async_copy(source, target, edge_sem.at[n])
+        for n, (source, target) in enumerate(
+            ((xr_in, xr_ref), (xl_in, xl_ref), (zr_in, zr_ref), (zl_in, zl_ref), (cz_in, cz_ref))
+        )
+    ]
+    loads, stores = [], []
+    for c in range(chunks):
+        at = pl.ds(c * CHUNK, CHUNK)
+        ends = (
+            (part_ref.at[:, at], out_ref.at[:, at]),
+            (rho_ref.at[at], state_ref.at[0, at]),
+            (mom_ref.at[:, at], state_ref.at[1:4, at]),
+            (en_ref.at[at], state_ref.at[4, at]),
+        )
+        loads.append([
+            pltpu.make_async_copy(source, target, load_sem.at[c, n])
+            for n, (source, target) in enumerate(ends)
+        ])
+        ends = ((out_ref.at[:, at], out_out.at[:, at]), (state_ref.at[:, at], state_out.at[:, at]))
+        stores.append([
+            pltpu.make_async_copy(source, target, store_sem.at[c, n])
+            for n, (source, target) in enumerate(ends)
+        ])
+    for copy in edges + sum(loads, []):
+        copy.start()
+    for copy in edges:
+        copy.wait()
     stack_ref[12:16] = jnp.zeros((4, stack_ref.shape[1]), jnp.float32)
-    dz = lax.dot_general(
-        stack_ref[...].astype(jnp.bfloat16), cz_ref[...], (((0,), (0,)), ((), ())),
-        preferred_element_type=jnp.float32,
-    )
-    dz_ref[...] = dz.reshape(dz_ref.shape)
-    left = (-SUM_COEF * w_ref[c, 0]) * xr_ref[0]
-    right = (SUM_COEF * w_ref[c, 1]) * xl_ref[0]
-    for i in range(CHUNK):
-        fresh = part_ref[:, i] + dz_ref[:, i]
-        fresh += ROOT**i * left + ROOT ** (CHUNK - 1 - i) * right
-        if i == 0:
-            fresh -= (DIFF_COEF * w_ref[c, 2]) * xr_ref[1]
-        if i == CHUNK - 1:
-            fresh += (DIFF_COEF * w_ref[c, 3]) * xl_ref[1]
-        out_ref[:, i] = fresh
-        scaled = (15.0 / 16.0) * fresh
-        state_ref[0, i] = rho_ref[i] + scaled[0]
-        for k in range(3):
-            state_ref[k + 1, i] = mom_ref[k, i] + scaled[k + 1]
-        state_ref[4, i] = en_ref[i] + scaled[4]
+    for c in range(chunks):
+        zr = zr_ref[c]
+        zl = zl_ref[c]
+        zr_high = zr.astype(jnp.bfloat16).astype(jnp.float32)
+        zl_high = zl.astype(jnp.bfloat16).astype(jnp.float32)
+        stack_ref[0:2] = zr_high
+        stack_ref[2:4] = zl_high
+        stack_ref[4:6] = zr - zr_high
+        stack_ref[6:8] = zl - zl_high
+        stack_ref[8:10] = zr_high
+        stack_ref[10:12] = zl_high
+        dz = lax.dot_general(
+            stack_ref[...].astype(jnp.bfloat16), cz_ref[...], (((0,), (0,)), ((), ())),
+            preferred_element_type=jnp.float32,
+        )
+        dz_ref[...] = dz.reshape(dz_ref.shape)
+        left = (-SUM_COEF * w_ref[c, 0]) * xr_ref[0]
+        right = (SUM_COEF * w_ref[c, 1]) * xl_ref[0]
+        for copy in loads[c]:
+            copy.wait()
+        for i in range(CHUNK):
+            row = c * CHUNK + i
+            fresh = out_ref[:, row] + dz_ref[:, i]
+            fresh += ROOT**i * left + ROOT ** (CHUNK - 1 - i) * right
+            if row == 0:
+                fresh -= DIFF_COEF * xr_ref[1]
+            if row == chunks * CHUNK - 1:
+                fresh += DIFF_COEF * xl_ref[1]
+            out_ref[:, row] = fresh
+            state_ref[:, row] = state_ref[:, row] + (15.0 / 16.0) * fresh
+        for copy in stores[c]:
+            copy.start()
+    for copy in sum(stores, []):
+        copy.wait()
 
 
 def per_device(density, momentum, energy, register):
@@ -251,18 +316,13 @@
     f32, bf16 = jnp.float32, jnp.bfloat16
     table = lambda shape: pl.BlockSpec(shape, lambda c: (0,) * len(shape))
     smem = pl.BlockSpec(memory_space=pltpu.SMEM)
+    hbm = pl.BlockSpec(memory_space=pl.ANY)
     weights = jnp.asarray(weight_table(chunks))
-    params = functools.partial(
-        pltpu.CompilerParams,
-        dimension_semantics=("arbitrary",),
-        vmem_limit_bytes=60 * 1024 * 1024,
-    )
     edge_x = (2, 5, ny, nz)
     edge_z = (chunks, 2, 5 * rows)
     buffers = [pltpu.VMEM(edge_x, f32)] * 2 + [pltpu.VMEM(edge_z, f32)] * 2
     high, low = local_table(nz)
 
-    ahead = lambda s: jnp.minimum(s, chunks - 1)
     back = lambda s: jnp.minimum(2 * chunks - 1 - s, chunks - 1)
     quint = pl.BlockSpec((5, CHUNK, ny, nz), lambda s: (0, back(s), 0, 0))
     part, xr, xl, zr, zl = pl.pallas_call(
@@ -270,10 +330,7 @@
         grid=(2 * chunks,),
         in_specs=[
             smem,
-            pl.BlockSpec((CHUNK, ny, nz), lambda s: (ahead(s), 0, 0)),
-            pl.BlockSpec((3, CHUNK, ny, nz), lambda s: (0, ahead(s), 0, 0)),
-            pl.BlockSpec((CHUNK, ny, nz), lambda s: (ahead(s), 0, 0)),
-            quint, table((16, nz)), table((nz, nz)), table((nz, nz)),
+            hbm, hbm, hbm, hbm, table((16, nz)), hbm, hbm,
         ],
         out_specs=[quint, table(edge_x), table(edge_x), table(edge_z), table(edge_z)],
         out_shape=[
@@ -288,34 +345,43 @@
             pltpu.VMEM((chunks, 5 * rows, nz), bf16),
             pltpu.VMEM((5, CHUNK, ny, nz), f32),
             pltpu.VMEM((5, ny, nz), f32),
+            pltpu.VMEM((5, nx, ny, nz), f32),
+            pltpu.VMEM((5, nx, ny, nz), f32),
+            pltpu.VMEM((nz, nz), bf16),
+            pltpu.VMEM((nz, nz), bf16),
             pltpu.SemaphoreType.DMA((4,)),
             pltpu.SemaphoreType.DMA((4,)),
+            pltpu.SemaphoreType.DMA((chunks, 4)),
+            pltpu.SemaphoreType.DMA((2,)),
         ],
-        compiler_params=params(collective_id=0, has_side_effects=True),
+        compiler_params=pltpu.CompilerParams(
+            dimension_semantics=("arbitrary",),
+            vmem_limit_bytes=60 * 1024 * 1024,
+            collective_id=0,
+            has_side_effects=True,
+        ),
         name="local_part",
     )(
         weights, density, momentum, energy, register,
         jnp.asarray(summary_table(nz)), jnp.asarray(high), jnp.asarray(low),
     )
 
-    plane = pl.BlockSpec((CHUNK, ny, nz), lambda c: (c, 0, 0))
-    triple = pl.BlockSpec((3, CHUNK, ny, nz), lambda c: (0, c, 0, 0))
-    quint = pl.BlockSpec((5, CHUNK, ny, nz), lambda c: (0, c, 0, 0))
-    line_z = pl.BlockSpec((1, 2, 5 * rows), lambda c: (c, 0, 0))
     return pl.pallas_call(
         final_kernel,
-        grid=(chunks,),
-        in_specs=[
-            smem, plane, triple, plane, quint, table(edge_x), table(edge_x),
-            line_z, line_z, table((16, nz)),
-        ],
-        out_specs=[quint, quint],
+        in_specs=[smem] + [hbm] * 9,
+        out_specs=[hbm, hbm],
         out_shape=[jax.ShapeDtypeStruct((5, nx, ny, nz), f32)] * 2,
-        scratch_shapes=[
+        scratch_shapes=[pltpu.VMEM((5, nx, ny, nz), f32)] * 2
+        + buffers
+        + [
+            pltpu.VMEM((16, nz), bf16),
             pltpu.VMEM((16, 5 * rows), f32),
             pltpu.VMEM((5, CHUNK, ny, nz), f32),
+            pltpu.SemaphoreType.DMA((5,)),
+            pltpu.SemaphoreType.DMA((chunks, 4)),
+            pltpu.SemaphoreType.DMA((chunks, 2)),
         ],
-        compiler_params=params(),
+        compiler_params=pltpu.CompilerParams(vmem_limit_bytes=60 * 1024 * 1024),
         name="neighbour_part",
     )(
         weights, density, momentum, energy, part, xr, xl, zr, zl,

time: 18.9 us -> 19.3 us (1.021)
  Pallas kernels: 17.9 us -> 18.4 us
    pallas_call x2, Pallas kernels: 17.9 us -> 18.4 us  [the longest x1 11.9 us: per_device(): pl.pallas_call(local_kernel, grid=(2 * chunks,), in_specs=[smem, hbm, hbm...]
where the time goes in v4:
time: 19.3 us; the launch traced here: 19 us
  Pallas kernels  18.4 us (95%)
  between operations  0.64 us (3%)
    pallas_call x1, Pallas kernels, per_device(): pl.pallas_call(local_kernel, grid=(2 * chunks,), in_specs=[smem, hbm, hbm...  11.9 us
    pallas_call x1, Pallas kernels, per_device(): pl.pallas_call(final_kernel, in_specs=[smem] + [hbm] * 9, out_specs=[hbm,...  6.51 us

profile of v4, /device:TPU:0, one launch (start us, length us, event | category | flops | bytes accessed | tf_op | source)
XLA Modules:
  0.0 19.0 jit_solution(6758655289641240177)
XLA Ops:
  0.6 11.9 %local_part.1 = (f32[5,64,8,256]{3,2,1,0:T(8,128)}, f32[2,5,8,256]{3,2,1,0:T(8,128)}, f32[2,5,8,256]{3,2,1,0:T(8,128)}, f32[4,2,640]{2,1,0:T(2,128)}, f32[4,2,640]{2,1,0:T(2,128)}) custom-call(f32[4,4]{1,0:T(4,128)} %constant.10.clone.w_ref, f32[64,8,256]{2,1,0:T(8,128)} %rho_ref.3, f32[3,64,8,256]{3,2,1,0:T(8,128)} %mom_ref.3, f32[64,8,256]{2,1,0:T(8,128)} %en_ref.3, ...), custom_call_target="tpu_custom_call" | custom-call | tf_op jit(solution)/shard_map/local_part/pallas_call | solution.py:328
  12.5 6.5 %neighbour_part.1 = (f32[5,64,8,256]{3,2,1,0:T(8,128)}, f32[5,64,8,256]{3,2,1,0:T(8,128)}) custom-call(f32[4,4]{1,0:T(4,128)} %constant.10.clone.w_ref, f32[64,8,256]{2,1,0:T(8,128)} %rho_ref.3, f32[3,64,8,256]{3,2,1,0:T(8,128)} %mom_ref.3, f32[64,8,256]{2,1,0:T(8,128)} %en_ref.3, f32[5,64,8,256]{3,2,1,0:T(8,128)} %get-tuple-element.7.part_ref, ...), custom_call_target="tpu_custom_call" | custom-call | tf_op jit(solution)/shard_map/neighbour_part/pallas_call | solution.py:369

commit v5 on v4

--- a/solution.py
+++ b/solution.py
@@ -62,16 +62,6 @@
     return split(np.sign(offset) * values)
 
 
-def weight_table(chunks):
-    out = np.zeros((chunks, 4), np.float32)
-    for c in range(chunks):
-        out[c, 0] = ROOT ** (c * CHUNK)
-        out[c, 1] = ROOT ** ((chunks - 1 - c) * CHUNK)
-        out[c, 2] = 1.0 if c == 0 else 0.0
-        out[c, 3] = 1.0 if c == chunks - 1 else 0.0
-    return out
-
-
 def fluxes(rho, mx, my, mz, energy):
     inverse = 1.0 / rho
     vx = mx * inverse
@@ -84,13 +74,12 @@
 
 
 def local_kernel(
-    w_ref, rho_ref, mom_ref, en_ref, reg_ref, zw_ref, hh_ref, hl_ref,
-    part_ref, xr_out, xl_out, zr_out, zl_out,
+    rho_ref, mom_ref, en_ref, reg_ref, zw_ref, hh_ref, hl_ref, cz_ref,
+    part_ref, cell_ref, xr_out, xl_out, zr_out, zl_out, cz_out,
     xr_ref, xl_ref, zr_ref, zl_ref, xr_got, xl_got, zr_got, zl_got,
     fx_ref, left_ref, high_ref, low_ref, dz_ref, carry_ref,
-    cell_ref, reg_buf, hh_buf, hl_buf, send_sem, recv_sem, load_sem, table_sem,
+    reg_buf, hh_buf, hl_buf, zw_buf, send_sem, recv_sem, load_sem, table_sem,
 ):
-    step = pl.program_id(0)
     chunks = high_ref.shape[0]
     cells, width, lanes = fx_ref.shape[0] - 2, fx_ref.shape[2], fx_ref.shape[3]
     rows = CHUNK * width
@@ -120,13 +109,16 @@
         return (
             pltpu.make_async_copy(hh_ref, hh_buf, table_sem.at[0]),
             pltpu.make_async_copy(hl_ref, hl_buf, table_sem.at[1]),
+            pltpu.make_async_copy(cz_ref, cz_out, table_sem.at[2]),
         )
 
-    @pl.when(step == 0)
-    def _():
+    zw_load = pltpu.make_async_copy(zw_ref, zw_buf, table_sem.at[3])
+
+    def enter():
         for chunk in range(chunks):
             for copy in loads_of(chunk, 0, 3):
                 copy.start()
+        zw_load.start()
         for copy in table_loads():
             copy.start()
         for chunk in range(chunks - 1, -1, -1):
@@ -141,8 +133,7 @@
         fx_ref[0] = jnp.zeros((5, width, lanes), jnp.float32)
         fx_ref[cells + 1] = jnp.zeros((5, width, lanes), jnp.float32)
 
-    @pl.when(step < chunks)
-    def _():
+    def forward(step, weight):
         start = step * CHUNK
         for copy in loads_of(step, 0, 3):
             copy.wait()
@@ -173,15 +164,16 @@
                 low_ref[step, at : at + 2 * width] = low
         for k in range(5):
             xr_ref[0, k] = left[k]
-            xl_ref[0, k] = xl_ref[0, k] + w_ref[step, 0] * right[k]
-            xl_ref[1, k] = xl_ref[1, k] + w_ref[step, 2] * first[k]
+            xl_ref[0, k] = xl_ref[0, k] + weight * right[k]
+            xl_ref[1, k] = xl_ref[1, k] + jnp.where(step == 0, 1.0, 0.0) * first[k]
         dims = (((1,), (1,)), ((), ()))
-        zw = zw_ref[...]
+        zw = zw_buf[...]
         one = lax.dot_general(zw, high_ref[step], dims, preferred_element_type=jnp.float32)
         two = lax.dot_general(zw, low_ref[step], dims, preferred_element_type=jnp.float32)
         total = one[0:4] + one[4:8] + two[0:4]
         zr_ref[step] = total[0:2]
         zl_ref[step] = total[2:4]
+        return weight * (ROOT**CHUNK)
 
     def copy_of(n):
         return pltpu.make_async_remote_copy(
@@ -193,21 +185,14 @@
             device_id_type=pl.DeviceIdType.MESH,
         )
 
-    @pl.when(step == chunks - 1)
-    def _():
+    def send():
         pl.semaphore_wait(barrier, 4)
         for n in range(4):
             copy_of(n).start()
 
-    @pl.when(step >= chunks)
-    def _():
+    def backward(step, none):
         chunk = 2 * chunks - 1 - step
         start = chunk * CHUNK
-
-        @pl.when(step == chunks)
-        def _():
-            for copy in table_loads():
-                copy.wait()
 
         loads_of(chunk, 3, 4)[0].wait()
         high = high_ref[chunk]
@@ -222,56 +207,41 @@
         for i in range(CHUNK - 1, -1, -1):
             lower = fx_ref[start + i]
             rate = SUM_COEF * (right - left_ref[start + i]) + DIFF_COEF * (upper - lower)
-            part_ref[:, i] = rate + dz_ref[:, i] - (5.0 / 9.0) * reg_buf[:, start + i]
+            part_ref[:, start + i] = rate + dz_ref[:, i] - (5.0 / 9.0) * reg_buf[:, start + i]
             right = here + ROOT * right
             upper = here
             here = lower
         carry_ref[...] = right
-
-    @pl.when(step == 2 * chunks - 1)
-    def _():
-        for n in range(4):
-            copy_of(n).wait()
-        xr_out[...] = xr_got[...]
-        xl_out[...] = xl_got[...]
-        zr_out[...] = zr_got[...]
-        zl_out[...] = zl_got[...]
+        return none
+
+    enter()
+    zw_load.wait()
+    lax.fori_loop(0, chunks, forward, jnp.float32(1.0))
+    send()
+    for copy in table_loads():
+        copy.wait()
+    lax.fori_loop(chunks, 2 * chunks, backward, 0)
+    for n in range(4):
+        copy_of(n).wait()
+    xr_out[...] = xr_got[...]
+    xl_out[...] = xl_got[...]
+    zr_out[...] = zr_got[...]
+    zl_out[...] = zl_got[...]
 
 
 def final_kernel(
-    w_ref, rho_ref, mom_ref, en_ref, part_ref, xr_in, xl_in, zr_in, zl_in, cz_in,
-    state_out, out_out, state_ref, out_ref, xr_ref, xl_ref, zr_ref, zl_ref, cz_ref,
-    stack_ref, dz_ref, edge_sem, load_sem, store_sem,
+    part_ref, cell_ref, xr_ref, xl_ref, zr_ref, zl_ref, cz_ref,
+    state_out, out_out, state_ref, out_ref, stack_ref, dz_ref, store_sem,
 ):
     chunks = zr_ref.shape[0]
-    edges = [
-        pltpu.make_async_copy(source, target, edge_sem.at[n])
-        for n, (source, target) in enumerate(
-            ((xr_in, xr_ref), (xl_in, xl_ref), (zr_in, zr_ref), (zl_in, zl_ref), (cz_in, cz_ref))
-        )
-    ]
-    loads, stores = [], []
+    stores = []
     for c in range(chunks):
         at = pl.ds(c * CHUNK, CHUNK)
-        ends = (
-            (part_ref.at[:, at], out_ref.at[:, at]),
-            (rho_ref.at[at], state_ref.at[0, at]),
-            (mom_ref.at[:, at], state_ref.at[1:4, at]),
-            (en_ref.at[at], state_ref.at[4, at]),
-        )
-        loads.append([
-            pltpu.make_async_copy(source, target, load_sem.at[c, n])
-            for n, (source, target) in enumerate(ends)
-        ])
         ends = ((out_ref.at[:, at], out_out.at[:, at]), (state_ref.at[:, at], state_out.at[:, at]))
         stores.append([
             pltpu.make_async_copy(source, target, store_sem.at[c, n])
             for n, (source, target) in enumerate(ends)
         ])
-    for copy in edges + sum(loads, []):
-        copy.start()
-    for copy in edges:
-        copy.wait()
     stack_ref[12:16] = jnp.zeros((4, stack_ref.shape[1]), jnp.float32)
     for c in range(chunks):
         zr = zr_ref[c]
@@ -289,20 +259,18 @@
             preferred_element_type=jnp.float32,
         )
         dz_ref[...] = dz.reshape(dz_ref.shape)
-        left = (-SUM_COEF * w_ref[c, 0]) * xr_ref[0]
-        right = (SUM_COEF * w_ref[c, 1]) * xl_ref[0]
-        for copy in loads[c]:
-            copy.wait()
+        left = (-SUM_COEF * ROOT ** (c * CHUNK)) * xr_ref[0]
+        right = (SUM_COEF * ROOT ** ((chunks - 1 - c) * CHUNK)) * xl_ref[0]
         for i in range(CHUNK):
             row = c * CHUNK + i
-            fresh = out_ref[:, row] + dz_ref[:, i]
+            fresh = part_ref[:, row] + dz_ref[:, i]
             fresh += ROOT**i * left + ROOT ** (CHUNK - 1 - i) * right
             if row == 0:
                 fresh -= DIFF_COEF * xr_ref[1]
             if row == chunks * CHUNK - 1:
                 fresh += DIFF_COEF * xl_ref[1]
             out_ref[:, row] = fresh
-            state_ref[:, row] = state_ref[:, row] + (15.0 / 16.0) * fresh
+            state_ref[:, row] = cell_ref[:, row] + (15.0 / 16.0) * fresh
         for copy in stores[c]:
             copy.start()
     for copy in sum(stores, []):
@@ -314,29 +282,24 @@
     chunks = nx // CHUNK
     rows = CHUNK * ny
     f32, bf16 = jnp.float32, jnp.bfloat16
-    table = lambda shape: pl.BlockSpec(shape, lambda c: (0,) * len(shape))
-    smem = pl.BlockSpec(memory_space=pltpu.SMEM)
+    vmem = pl.BlockSpec(memory_space=pltpu.VMEM)
     hbm = pl.BlockSpec(memory_space=pl.ANY)
-    weights = jnp.asarray(weight_table(chunks))
+    far = lambda value: pltpu.with_memory_space_constraint(value, pltpu.HBM)
+    close = lambda value: pltpu.with_memory_space_constraint(value, pltpu.VMEM)
     edge_x = (2, 5, ny, nz)
     edge_z = (chunks, 2, 5 * rows)
+    full = (5, nx, ny, nz)
     buffers = [pltpu.VMEM(edge_x, f32)] * 2 + [pltpu.VMEM(edge_z, f32)] * 2
     high, low = local_table(nz)
 
-    back = lambda s: jnp.minimum(2 * chunks - 1 - s, chunks - 1)
-    quint = pl.BlockSpec((5, CHUNK, ny, nz), lambda s: (0, back(s), 0, 0))
-    part, xr, xl, zr, zl = pl.pallas_call(
+    kept = pl.pallas_call(
         local_kernel,
-        grid=(2 * chunks,),
-        in_specs=[
-            smem,
-            hbm, hbm, hbm, hbm, table((16, nz)), hbm, hbm,
-        ],
-        out_specs=[quint, table(edge_x), table(edge_x), table(edge_z), table(edge_z)],
+        in_specs=[hbm] * 8,
+        out_specs=[vmem] * 7,
         out_shape=[
-            jax.ShapeDtypeStruct(shape, f32)
-            for shape in ((5, nx, ny, nz), edge_x, edge_x, edge_z, edge_z)
-        ],
+            pltpu.VMEM(shape, f32) for shape in (full, full, edge_x, edge_x, edge_z, edge_z)
+        ]
+        + [pltpu.VMEM((16, nz), bf16)],
         scratch_shapes=buffers * 2
         + [
             pltpu.VMEM((nx + 2, 5, ny, nz), f32),
@@ -345,48 +308,39 @@
             pltpu.VMEM((chunks, 5 * rows, nz), bf16),
             pltpu.VMEM((5, CHUNK, ny, nz), f32),
             pltpu.VMEM((5, ny, nz), f32),
-            pltpu.VMEM((5, nx, ny, nz), f32),
-            pltpu.VMEM((5, nx, ny, nz), f32),
+            pltpu.VMEM(full, f32),
             pltpu.VMEM((nz, nz), bf16),
             pltpu.VMEM((nz, nz), bf16),
+            pltpu.VMEM((16, nz), bf16),
             pltpu.SemaphoreType.DMA((4,)),
             pltpu.SemaphoreType.DMA((4,)),
             pltpu.SemaphoreType.DMA((chunks, 4)),
-            pltpu.SemaphoreType.DMA((2,)),
+            pltpu.SemaphoreType.DMA((4,)),
         ],
         compiler_params=pltpu.CompilerParams(
-            dimension_semantics=("arbitrary",),
-            vmem_limit_bytes=60 * 1024 * 1024,
-            collective_id=0,
-            has_side_effects=True,
+            vmem_limit_bytes=36 * 1024 * 1024, collective_id=0, has_side_effects=True
         ),
         name="local_part",
     )(
-        weights, density, momentum, energy, register,
-        jnp.asarray(summary_table(nz)), jnp.asarray(high), jnp.asarray(low),
+        far(density), far(momentum), far(energy), far(register),
+        far(jnp.asarray(summary_table(nz))), far(jnp.asarray(high)), far(jnp.asarray(low)),
+        far(jnp.asarray(correction_table(nz))),
     )
 
     return pl.pallas_call(
         final_kernel,
-        in_specs=[smem] + [hbm] * 9,
+        in_specs=[vmem] * 7,
         out_specs=[hbm, hbm],
-        out_shape=[jax.ShapeDtypeStruct((5, nx, ny, nz), f32)] * 2,
-        scratch_shapes=[pltpu.VMEM((5, nx, ny, nz), f32)] * 2
-        + buffers
+        out_shape=[jax.ShapeDtypeStruct(full, f32)] * 2,
+        scratch_shapes=[pltpu.VMEM(full, f32)] * 2
         + [
-            pltpu.VMEM((16, nz), bf16),
             pltpu.VMEM((16, 5 * rows), f32),
             pltpu.VMEM((5, CHUNK, ny, nz), f32),
-            pltpu.SemaphoreType.DMA((5,)),
-            pltpu.SemaphoreType.DMA((chunks, 4)),
             pltpu.SemaphoreType.DMA((chunks, 2)),
         ],
-        compiler_params=pltpu.CompilerParams(vmem_limit_bytes=60 * 1024 * 1024),
+        compiler_params=pltpu.CompilerParams(vmem_limit_bytes=36 * 1024 * 1024),
         name="neighbour_part",
-    )(
-        weights, density, momentum, energy, part, xr, xl, zr, zl,
-        jnp.asarray(correction_table(nz)),
-    )
+    )(*(close(value) for value in kept))
 
 
 def solution(mesh):

time: 19.3 us -> 14.2 us (0.74)
  Pallas kernels: 18.4 us -> 13.4 us
    pallas_call x2, Pallas kernels: 18.4 us -> 13.4 us  [the longest x1 10.4 us: per_device(): pl.pallas_call(local_kernel, in_specs=[hbm] * 8, out_specs=[vmem] * 7, ou...]
where the time goes in v5:
time: 14.2 us; the launch traced here: 14.1 us
  Pallas kernels  13.4 us (94%)
  between operations  0.64 us (5%)
    pallas_call x1, Pallas kernels, per_device(): pl.pallas_call(local_kernel, in_specs=[hbm] * 8, out_specs=[vmem] * 7, ou...  10.4 us
    pallas_call x1, Pallas kernels, per_device(): pl.pallas_call(final_kernel, in_specs=[vmem] * 7, out_specs=[hbm, hbm], o...  3.01 us

profile of v5, /device:TPU:0, one launch (start us, length us, event | category | flops | bytes accessed | tf_op | source)
XLA Modules:
  0.0 14.1 jit_solution(10322815673272466219)
XLA Ops:
  0.6 10.4 %local_part.1 = (f32[5,64,8,256]{3,2,1,0:T(8,128)S(1)}, f32[5,64,8,256]{3,2,1,0:T(8,128)S(1)}, f32[2,5,8,256]{3,2,1,0:T(8,128)S(1)}, f32[2,5,8,256]{3,2,1,0:T(8,...) custom-call(f32[64,8,256]{2,1,0:T(8,128)} %rho_ref.1, ...), custom_call_target="tpu_custom_call" | custom-call | tf_op jit(solution)/shard_map/local_part/pallas_call | solution.py:295
  11.0 3.0 %neighbour_part.1 = (f32[5,64,8,256]{3,2,1,0:T(8,128)}, f32[5,64,8,256]{3,2,1,0:T(8,128)}) custom-call(f32[5,64,8,256]{3,2,1,0:T(8,128)S(1)} %get-tuple-element.9.part_ref, f32[5,64,8,256]{3,2,1,0:T(8,128)S(1)} %get-tuple-element.10.cell_ref, f32[2,5,8,256]{3,2,1,0:T(8,128)S(1)} %get-tuple-element.11.xr_ref, f32[2,5,8,256]{3,2,1,0:T(8,128)S(1)} %get-tuple-element.12.xl_ref, ...), custom_call_target="tpu_custom_call" | custom-call | tf_op jit(solution)/shard_map/neighbour_part/pallas_call | solution.py:330

commit v6 on v5

--- a/solution.py
+++ b/solution.py
@@ -119,10 +119,6 @@
             for copy in loads_of(chunk, 0, 3):
                 copy.start()
         zw_load.start()
-        for copy in table_loads():
-            copy.start()
-        for chunk in range(chunks - 1, -1, -1):
-            loads_of(chunk, 3, 4)[0].start()
         for target in neighbours:
             pl.semaphore_signal(
                 barrier, inc=1, device_id=target, device_id_type=pl.DeviceIdType.MESH
@@ -137,6 +133,14 @@
         start = step * CHUNK
         for copy in loads_of(step, 0, 3):
             copy.wait()
+
+        @pl.when(step == chunks // 2)
+        def _():
+            for copy in table_loads():
+                copy.start()
+            for chunk in range(chunks - 1, -1, -1):
+                loads_of(chunk, 3, 4)[0].start()
+
         left = [xr_ref[0, k] for k in range(5)]
         right = [None] * 5
         first = [None] * 5

time: 14.2 us -> 14.3 us (level)
  no operation moved by 1% of the time
where the time goes in v6:
time: 14.3 us; the launch traced here: 14 us
  Pallas kernels  13.4 us (94%)
  between operations  0.64 us (4%)
    pallas_call x1, Pallas kernels, per_device(): pl.pallas_call(local_kernel, in_specs=[hbm] * 8, out_specs=[vmem] * 7, ou...  10.4 us
    pallas_call x1, Pallas kernels, per_device(): pl.pallas_call(final_kernel, in_specs=[vmem] * 7, out_specs=[hbm, hbm], o...  2.99 us

profile of v6, /device:TPU:0, one launch (start us, length us, event | category | flops | bytes accessed | tf_op | source)
XLA Modules:
  0.0 14.0 jit_solution(14938303212387288878)
XLA Ops:
  0.6 10.4 %local_part.1 = (f32[5,64,8,256]{3,2,1,0:T(8,128)S(1)}, f32[5,64,8,256]{3,2,1,0:T(8,128)S(1)}, f32[2,5,8,256]{3,2,1,0:T(8,128)S(1)}, f32[2,5,8,256]{3,2,1,0:T(8,...) custom-call(f32[64,8,256]{2,1,0:T(8,128)} %rho_ref.1, ...), custom_call_target="tpu_custom_call" | custom-call | tf_op jit(solution)/shard_map/local_part/pallas_call | solution.py:299
  11.0 3.0 %neighbour_part.1 = (f32[5,64,8,256]{3,2,1,0:T(8,128)}, f32[5,64,8,256]{3,2,1,0:T(8,128)}) custom-call(f32[5,64,8,256]{3,2,1,0:T(8,128)S(1)} %get-tuple-element.9.part_ref, f32[5,64,8,256]{3,2,1,0:T(8,128)S(1)} %get-tuple-element.10.cell_ref, f32[2,5,8,256]{3,2,1,0:T(8,128)S(1)} %get-tuple-element.11.xr_ref, f32[2,5,8,256]{3,2,1,0:T(8,128)S(1)} %get-tuple-element.12.xl_ref, ...), custom_call_target="tpu_custom_call" | custom-call | tf_op jit(solution)/shard_map/neighbour_part/pallas_call | solution.py:334

commit v7 on v5

--- a/solution.py
+++ b/solution.py
@@ -216,11 +216,11 @@
 
     enter()
     zw_load.wait()
-    lax.fori_loop(0, chunks, forward, jnp.float32(1.0))
+    lax.fori_loop(0, chunks, forward, jnp.float32(1.0), unroll=True)
     send()
     for copy in table_loads():
         copy.wait()
-    lax.fori_loop(chunks, 2 * chunks, backward, 0)
+    lax.fori_loop(chunks, 2 * chunks, backward, 0, unroll=True)
     for n in range(4):
         copy_of(n).wait()
     xr_out[...] = xr_got[...]

time: 14.2 us -> 14.1 us (level)
  no operation moved by 1% of the time
where the time goes in v7:
time: 14.1 us; the launch traced here: 14 us
  Pallas kernels  13.4 us (95%)
  between operations  0.64 us (5%)
    pallas_call x1, Pallas kernels, per_device(): pl.pallas_call(local_kernel, in_specs=[hbm] * 8, out_specs=[vmem] * 7, ou...  10.4 us
    pallas_call x1, Pallas kernels, per_device(): pl.pallas_call(final_kernel, in_specs=[vmem] * 7, out_specs=[hbm, hbm], o...  3 us

profile of v7, /device:TPU:0, one launch (start us, length us, event | category | flops | bytes accessed | tf_op | source)
XLA Modules:
  0.0 14.0 jit_solution(8422412146980742798)
XLA Ops:
  0.6 10.4 %local_part.1 = (f32[5,64,8,256]{3,2,1,0:T(8,128)S(1)}, f32[5,64,8,256]{3,2,1,0:T(8,128)S(1)}, f32[2,5,8,256]{3,2,1,0:T(8,128)S(1)}, f32[2,5,8,256]{3,2,1,0:T(8,...) custom-call(f32[64,8,256]{2,1,0:T(8,128)} %rho_ref.1, ...), custom_call_target="tpu_custom_call" | custom-call | tf_op jit(solution)/shard_map/local_part/pallas_call | solution.py:295
  11.0 3.0 %neighbour_part.1 = (f32[5,64,8,256]{3,2,1,0:T(8,128)}, f32[5,64,8,256]{3,2,1,0:T(8,128)}) custom-call(f32[5,64,8,256]{3,2,1,0:T(8,128)S(1)} %get-tuple-element.9.part_ref, f32[5,64,8,256]{3,2,1,0:T(8,128)S(1)} %get-tuple-element.10.cell_ref, f32[2,5,8,256]{3,2,1,0:T(8,128)S(1)} %get-tuple-element.11.xr_ref, f32[2,5,8,256]{3,2,1,0:T(8,128)S(1)} %get-tuple-element.12.xl_ref, ...), custom_call_target="tpu_custom_call" | custom-call | tf_op jit(solution)/shard_map/neighbour_part/pallas_call | solution.py:330
